TPU v7x, 32 devices: a whole 2x2x4 slice. The times are simulated.
32 devices in a mesh: row: 4 (over z), col: 8 (over y, x, core).
Axes of the slice: x: 2, y: 2, z: 4, core: 2. Of those that a mesh axis runs over, the one named last changes fastest.
Arguments:
- tokens: bfloat16 [2048, 2048], P('col', 'row'), may hold values from -6 to 6
- router: bfloat16 [2048, 16], replicated, may hold values from -0.125 to 0.125
- shared_gate_vector: bfloat16 [2048], replicated, may hold values from -0.125 to 0.125
- shared_gate_weight: bfloat16 [2048, 5632], P('col', 'row'), may hold values from -0.125 to 0.125
- shared_up_weight: bfloat16 [2048, 5632], P('col', 'row'), may hold values from -0.125 to 0.125
- shared_down_weight: bfloat16 [5632, 2048], P('row', 'col'), may hold values from -0.078125 to 0.078125
- routed_gate_weight: bfloat16 [16, 2048, 1408], P('col', None, 'row'), may hold values from -0.125 to 0.125
- routed_up_weight: bfloat16 [16, 2048, 1408], P('col', None, 'row'), may hold values from -0.125 to 0.125
- routed_down_weight: bfloat16 [16, 1408, 2048], P('col', 'row'), may hold values from -0.15625 to 0.15625
- adapter_input_factor: bfloat16 [64, 16, 2048], P(None, None, 'row'), may hold values from -0.125 to 0.125
- adapter_output_factor: bfloat16 [64, 16, 5632], P(None, None, 'row'), may hold values from -0.29882812 to 0.29882812
- routes: int32 [2048, 4], P('col'), may hold values from 0 to 15, all different within a row; in each aligned block of 256 rows (0 to 255, 256 to 511, ...) at most 128 rows name the same one
- lengths: int32 [8, 16], P('col'), may hold values from 1 to 128, 256 in all within a row
- prompt_adapter_index: int32 [8, 16], P('col'), may hold values from 0 to 15
- active_adapter_index: int32 [16], replicated, may hold values from 0 to 63, as said below
Outputs:
- moe_out: float32 [2048, 2048], P('col', 'row')
Inputs may be any that keep to these rules, and one draw needn't show every extreme that they name: `routes`: in each group of 256 consecutive tokens no expert is named by more than 128 tokens, a bound that some block reaches. Each group's 16 lengths sum to 256; the longest is exactly 128. `active_adapter_index`: the 16 entries are distinct.
All inputs are finite; a program needn't handle non-finite values.
Results may differ from a plain program's by a relative error of at most 0.003.
Values may be sent and summed in bfloat16 or wider, within the bound.
A program may use at most 128 MiB of HBM per device.

v0:
```python
import jax
import jax.numpy as jnp
from jax import lax
from jax.sharding import PartitionSpec as P

ADAPTER_SCALE = 2.0


def on_device(
    tokens,
    router,
    shared_gate_vector,
    shared_gate_weight,
    shared_up_weight,
    shared_down_weight,
    routed_gate_weight,
    routed_up_weight,
    routed_down_weight,
    adapter_input_factor,
    adapter_output_factor,
    routes,
    lengths,
    prompt_adapter_index,
    active_adapter_index,
):
    all_features = lax.all_gather(tokens, "row", axis=1, tiled=True)
    token_count = all_features.shape[0]
    full_width = all_features.shape[1]
    local_width = tokens.shape[1]
    col_count = lax.axis_size("col")
    local_experts = routed_gate_weight.shape[0]
    expert_count = local_experts * col_count
    route_count = routes.shape[1]
    capacity = 2 * token_count * route_count // expert_count
    logits = jnp.dot(all_features, router, preferred_element_type=jnp.float32)
    onehot = routes[:, :, None] == jnp.arange(expert_count, dtype=jnp.int32)[None, None, :]
    picked = jnp.sum(jnp.where(onehot, logits[:, None, :], 0.0), axis=2)
    raw_exp = jnp.exp(picked)
    gate_weights = raw_exp / jnp.sum(raw_exp, axis=1, keepdims=True)
    share = jax.nn.sigmoid(
        jnp.dot(all_features, shared_gate_vector, preferred_element_type=jnp.float32)
    )
    hit_table = jnp.any(onehot, axis=1).astype(jnp.int32)
    running_count = jnp.cumsum(hit_table, axis=0)
    slot_rank = running_count - hit_table
    route_rank = jnp.sum(jnp.where(onehot, slot_rank[:, None, :], 0), axis=2)
    row_index = routes * capacity + route_rank
    request_ends = jnp.cumsum(lengths[0])
    request_count = lengths.shape[1]
    token_position = jnp.arange(token_count, dtype=jnp.int32)
    request_of = jnp.sum(
        (token_position[:, None] >= request_ends[None, :]).astype(jnp.int32), axis=1
    )
    request_match = request_of[:, None] == jnp.arange(request_count, dtype=jnp.int32)[None, :]
    adapter_of = jnp.sum(jnp.where(request_match, prompt_adapter_index[0][None, :], 0), axis=1)
    picked_input_factor = jnp.take(adapter_input_factor, active_adapter_index, axis=0)
    rank_width = picked_input_factor.shape[1]
    reduced_rank_value = picked_input_factor.shape[0] * rank_width
    full_in = lax.all_gather(picked_input_factor, "row", axis=2, tiled=True).reshape(
        reduced_rank_value, full_width
    )
    low_rank = lax.dot_general(
        all_features, full_in, (((1,), (1,)), ((), ())), preferred_element_type=jnp.float32
    )
    owner = jnp.arange(reduced_rank_value, dtype=jnp.int32) // rank_width
    adapter_mask = adapter_of[:, None] == owner[None, :]
    low_masked = jnp.where(adapter_mask, low_rank.astype(jnp.bfloat16), jnp.zeros((), jnp.bfloat16))
    picked_output_factor = jnp.take(adapter_output_factor, active_adapter_index, axis=0).reshape(
        reduced_rank_value, adapter_output_factor.shape[2]
    )
    adapter_update = jnp.dot(low_masked, picked_output_factor, preferred_element_type=jnp.float32)
    shared_gate_value = jnp.dot(
        all_features,
        lax.all_gather(shared_gate_weight, "col", axis=0, tiled=True),
        preferred_element_type=jnp.float32,
    )
    shared_up_value = jnp.dot(
        all_features,
        lax.all_gather(shared_up_weight, "col", axis=0, tiled=True),
        preferred_element_type=jnp.float32,
    )
    shared_hidden_units = (
        jax.nn.silu(shared_gate_value) * (shared_up_value + ADAPTER_SCALE * adapter_update)
    ).astype(jnp.bfloat16)
    shared_part = jnp.dot(
        shared_hidden_units,
        lax.all_gather(shared_down_weight, "col", axis=1, tiled=True),
        preferred_element_type=jnp.float32,
    )
    shared_part = shared_part * share[:, None]
    positions = jnp.arange(capacity, dtype=jnp.int32)
    slot_token = jnp.sum(
        (running_count.T[:, None, :] <= positions[None, :, None]).astype(jnp.int32), axis=2
    )
    slot_valid = positions[None, :] < running_count[-1][:, None]
    picked_rows = jnp.take(all_features, jnp.minimum(slot_token, token_count - 1), axis=0)
    chosen = jnp.where(slot_valid[:, :, None], picked_rows, jnp.zeros((), jnp.bfloat16))
    outgoing = chosen.reshape(col_count, local_experts, capacity, full_width)
    slot_block = lax.all_to_all(outgoing, "col", split_axis=0, concat_axis=0, tiled=True)
    gate_part = jnp.einsum(
        "sexd,edf->sexf", slot_block, routed_gate_weight, preferred_element_type=jnp.float32
    )
    up_part = jnp.einsum(
        "sexd,edf->sexf", slot_block, routed_up_weight, preferred_element_type=jnp.float32
    )
    hidden = (jax.nn.silu(gate_part) * up_part).astype(jnp.bfloat16)
    partial_value = jnp.einsum(
        "sexf,efd->sexd", hidden, routed_down_weight, preferred_element_type=jnp.float32
    )
    summed, shared_sum = (
        lax.psum_scatter(partial_value, "row", scatter_dimension=3, tiled=True),
        lax.psum_scatter(shared_part, "row", scatter_dimension=1, tiled=True),
    )
    returned = lax.all_to_all(summed, "col", split_axis=0, concat_axis=0, tiled=True)
    flat_rows = returned.reshape(expert_count * capacity, local_width)
    routed_rows = jnp.take(flat_rows, row_index, axis=0)
    routed = jnp.sum(gate_weights[:, :, None] * routed_rows, axis=1)
    return routed + shared_sum


def solution(mesh):
    return jax.shard_map(
        on_device,
        mesh=mesh,
        in_specs=(
            P("col", "row"),
            P(),
            P(),
            P("col", "row"),
            P("col", "row"),
            P("row", "col"),
            P("col", None, "row"),
            P("col", None, "row"),
            P("col", "row", None),
            P(None, None, "row"),
            P(None, None, "row"),
            P("col", None),
            P("col", None),
            P("col", None),
            P(),
        ),
        out_specs=P("col", "row"),
        check_vma=False,
    )
```

profile of v0, /device:TPU:11, one launch (start us, length us, event | category | flops | bytes accessed | tf_op | source)
XLA Modules:
  0.0 617.7 jit_solution(3763265294672293814)
XLA Ops:
  6.5 0.7 all-gather.6.cloned.1.call-update
  7.3 0.0 all-gather.12.cloned.1.call-start
  7.3 0.8 compare_select_fusion.3
  8.1 1.8 gather_fusion.2
  9.9 0.7 compare_and_fusion.2
  10.5 0.8 broadcast_select_fusion
  11.3 0.0 all-gather.12.cloned.1.call-update
  11.4 0.0 all-gather.8.cloned.1.call-start
  11.4 0.7 all-gather.8.cloned.1.call-update
  12.1 0.0 all-gather.10.cloned.1.call-start
  12.1 0.5 all-gather.10.cloned.1.call-update
  12.7 0.0 all-gather.14.cloned.1.call-start
  12.7 0.5 all-gather.14.cloned.1.call-update
  13.3 0.0 reduce-scatter.3.cloned.1.call-start
  13.4 0.6 reduce-window.18
  13.9 0.2 slice_reduce_fusion
  14.2 0.1 fusion.33
  14.2 0.4 convert_reduce_fusion
  14.6 0.2 slice_reduce_fusion.1
  14.8 0.1 lt.58
  14.9 0.1 compare_and_fusion
  15.0 22.8 %all-gather.6.cloned.1.call-done = bf16[256,2048]{1,0:T(8,128)(2,1)} async-done(((bf16[256,512]{1,0:T(8,128)(2,1)}), bf16[256,2048]{1,0:T(8,128)(2,1)}) %all-gather.6.cloned.1.call-update) | async-done | bytes 1048592 | tf_op jit(solution)/shard_map/all_gather | solution.py:26
  37.8 17.7 %gather_fusion = bf16[2048,2048]{1,0:T(8,128)(2,1)} fusion(bf16[256,2048]{1,0:T(8,128)(2,1)} %all-gather.6.cloned.1.call-done, s32[2048]{0:T(1024)S(1)} %fusion.29), kind=kCustom, calls=%fused_computation | custom fusion | bytes 16785408 | tf_op jit(solution)/shard_map/jit(_take)/gather | solution.py:96
  55.5 4.7 select_select_fusion
  60.1 0.0 copy-start.9
  60.2 126.5 %all_to_all.10 = bf16[8,2,128,2048]{3,2,1,0:T(8,128)(2,1)S(1)} all-to-all(bf16[8,2,128,2048]{3,2,1,0:T(8,128)(2,1)S(1)} %select_select_fusion), channel_id=1, replica_groups=mesh['row'=4,'col'=8] {'col'}, dimensions={0} | all-to-all | bytes 16777216 | tf_op jit(solution)/shard_map/all_to_all | solution.py:99
  186.7 3.2 copy-done.3
  189.9 4.8 fusion.2
  194.7 14.2 %convolution_bitcast_fusion = f32[8,2,128,2048]{3,2,0,1:T(8,128)} fusion(bf16[2,352,2048]{2,1,0:T(8,128)(2,1)S(1)} %copy-done, f32[2,8,128,352]{2,3,1,0:T(8,128)} %fusion.2, bf16[2,2048,352]{1,2,0:T(8,128)(2,1)} %param.22, bf16[8,2,128,2048]{3,2,1,0:T(8,128)(2,1)} %copy-done.3), kind=kOutput, calls=%fused_computation.9 | convolution fusion | flops 5909905408 | bytes 33816576 | tf_op jit(solution)/shard_map/sexf,efd->sexd/dot_general | solution.py:107
  208.9 0.0 reduce-scatter.3.cloned.1.call-update
  208.9 0.2 reduce-scatter.5.cloned.1.call-start
  209.1 0.1 broadcast_in_dim.137
  209.2 0.1 broadcast_in_dim.138
  209.3 0.2 copy-done.6
  209.6 0.1 copy.54
  209.7 0.1 reduce.2
  209.8 2.6 gather_fusion.3
  212.4 0.1 convert_reduce_fusion.1
  212.5 0.1 select_reduce_fusion.2
  212.6 0.2 bitcast_select_fusion
  212.7 0.4 fusion.37
  213.1 0.0 all-gather.12.cloned.1.call-done
  213.2 1.7 fusion.24
  214.9 0.0 all-gather.8.cloned.1.call-done
  214.9 5.5 fusion.35
  220.4 6.0 fusion.36
  226.4 31.8 %all-gather.14.cloned.1.call-done = bf16[1408,2048]{1,0:T(8,128)(2,1)} async-done(((bf16[1408,256]{1,0:T(8,128)(2,1)}), bf16[1408,2048]{1,0:T(8,128)(2,1)}) %all-gather.14.cloned.1.call-update) | async-done | bytes 5767184 | tf_op jit(solution)/shard_map/all_gather | solution.py:87
  258.2 7.1 %convolution_multiply_fusion.1 = f32[256,2048]{1,0:T(8,128)} fusion(bf16[1408,2048]{1,0:T(8,128)(2,1)} %all-gather.14.cloned.1.call-done, f32[256,1408]{1,0:T(8,128)} %fusion.36, bf16[256,256]{0,1:T(8,128)(2,1)S(1)} %fusion.24, bf16[256,1408]{1,0:T(8,128)(2,1)S(1)} %bitcast_select_fusion, f32[256,1408]{1,0:T(8,128)} %fusion.35, f32[256]{0:T(256)S(1)} %add_divide_fusion), kind=kOutput, calls=%fused_computation.23 | convolution fusion | flops 1664352256 | bytes 11600896 | tf_op jit(solution)/shard_map/dot_general | solution.py:85
  265.3 0.0 reduce-scatter.5.cloned.1.call-update
  265.3 272.0 %reduce-scatter.3.cloned.1.call-done = f32[8,2,128,512]{3,2,0,1:T(8,128)} async-done(((f32[8,2,128,2048]{3,2,0,1:T(8,128)}), f32[8,2,128,512]{3,2,0,1:T(8,128)}) %reduce-scatter.3.cloned.1.call-update) | async-done | bytes 4194320 | tf_op jit(solution)/shard_map/reduce_scatter | solution.py:111
  537.3 4.8 copy.52
  542.1 5.2 all-to-all-start.1
  547.3 0.1 convert_subtract_fusion
  547.4 0.8 copy.49
  548.2 0.1 copy.53
  548.3 0.1 reshape.165
  548.5 0.4 fusion.34
  548.9 0.1 copy.46
  549.1 45.9 %all-to-all-done.1 = f32[8,2,128,512]{3,2,1,0:T(8,128)} async-done(((f32[8,2,128,512]{3,2,1,0:T(8,128)}), f32[8,2,128,512]{3,2,1,0:T(8,128)}, u32[]{:S(2)}, u32[]{:S(2)}) %all-to-all-start.1) | async-done | bytes 4194336 | tf_op jit(solution)/shard_map/all_to_all | solution.py:114
  594.9 7.5 %gather_fusion.1 = f32[1024,512]{1,0:T(8,128)} fusion(f32[2048,512]{1,0:T(8,128)} %bitcast.15, s32[1024]{0:T(1024)S(1)} %broadcast_clamp_fusion), kind=kCustom, calls=%fused_computation.1 | custom fusion | bytes 4198400 | tf_op jit(solution)/shard_map/jit(_take)/gather | solution.py:116
  602.4 3.0 reshape.164
  605.5 3.5 multiply_reduce_fusion
  608.9 0.0 reduce-scatter.5.cloned.1.call-done
  609.0 1.9 add.77
  (36 shorter events, 0.3 us)
Async XLA Ops:
  6.5 188.1 %copy-start = (bf16[2,352,2048]{2,1,0:T(8,128)(2,1)S(1)}, bf16[2,352,2048]{2,1,0:T(8,128)(2,1)}, u32[]{:S(2)}) copy-start(bf16[2,352,2048]{2,1,0:T(8,128)(2,1)} %param.23) | copy-start | bytes 8650756
  6.5 6.8 %copy-start.5 = (s32[256,4]{0,1:T(4,128)S(1)}, s32[256,4]{0,1:T(4,128)}, u32[]{:S(2)}) copy-start(s32[256,4]{0,1:T(4,128)} %param.26) | copy-start | bytes 12292
  6.5 31.2 %all-gather.6.cloned.1.call-start = ((), (), s32[]{:S(2)}) async-start(), calls=%async_computation.4 | async-start | bytes 1310720 | tf_op jit(solution)/shard_map/all_gather | solution.py:26
  7.3 205.9 %all-gather.12.cloned.1.call-start = ((), (), s32[]{:S(2)}) async-start(), calls=%async_computation.8 | async-start | bytes 1310720 | tf_op jit(solution)/shard_map/all_gather | solution.py:59
  11.4 203.5 %all-gather.8.cloned.1.call-start = ((), (), s32[]{:S(2)}) async-start(), calls=%async_computation.6 | async-start | bytes 6488064 | tf_op jit(solution)/shard_map/all_gather | solution.py:74
  12.1 208.3 %all-gather.10.cloned.1.call-start = ((), (), s32[]{:S(2)}) async-start(), calls=%async_computation.7 | async-start | bytes 6488064 | tf_op jit(solution)/shard_map/all_gather | solution.py:79
  12.7 245.5 %all-gather.14.cloned.1.call-start = ((), (), s32[]{:S(2)}) async-start(), calls=%async_computation.9 | async-start | bytes 6488064 | tf_op jit(solution)/shard_map/all_gather | solution.py:87
  13.3 524.1 %reduce-scatter.3.cloned.1.call-start = ((), (), s32[]{:S(2)}) async-start(), calls=%async_computation.5 | async-start | bytes 20971520 | tf_op jit(solution)/shard_map/reduce_scatter | solution.py:111
  60.1 129.7 %copy-start.9 = (bf16[2,2048,352]{1,2,0:T(8,128)(2,1)S(1)}, bf16[2,2048,352]{1,2,0:T(8,128)(2,1)}, u32[]{:S(2)}) copy-start(bf16[2,2048,352]{1,2,0:T(8,128)(2,1)} %param.21) | copy-start | bytes 8650756
  186.7 3.2 copy-start.3
  208.9 0.7 copy-start.6
  208.9 0.7 copy-start.7
  208.9 3.6 copy-start.8
  208.9 3.8 copy-start.2
  208.9 400.0 %reduce-scatter.5.cloned.1.call-start = ((), (), s32[]{:S(2)}) async-start(), calls=%async_computation.10 | async-start | bytes 2621440 | tf_op jit(solution)/shard_map/reduce_scatter | solution.py:112
  542.1 6.4 %copy-start.4 = (bf16[2048,16]{0,1:T(8,128)(2,1)S(1)}, bf16[2048,16]{0,1:T(8,128)(2,1)}, u32[]{:S(2)}) copy-start(bf16[2048,16]{0,1:T(8,128)(2,1)} %param.16) | copy-start | bytes 196612
  542.1 52.8 %all-to-all-start.1 = ((f32[8,2,128,512]{3,2,1,0:T(8,128)}), f32[8,2,128,512]{3,2,1,0:T(8,128)}, u32[]{:S(2)}, u32[]{:S(2)}) async-start(f32[8,2,128,512]{3,2,1,0:T(8,128)} %copy.52), calls=%async_computation.2 | async-start | bytes 8388608 | tf_op jit(solution)/shard_map/all_to_all | solution.py:114
  602.4 8.5 %copy-start.1 = (bf16[2,352,2048]{2,1,0:T(8,128)(2,1)S(1)}, bf16[2,352,2048]{2,1,0:T(8,128)(2,1)}, u32[]{:S(2)}) copy-start(bf16[2,352,2048]{2,1,0:T(8,128)(2,1)} %param.23) | copy-start | bytes 8650756
Sparse Core Ops, SparseCore 0:
  8.9 28.8 all-gather.5
  39.3 27.4 all-gather.11
  68.7 90.3 all-gather.7
  160.8 51.2 all-gather.9
  213.8 44.3 all-gather.13
  260.4 276.9 reduce-scatter.2
  539.7 45.1 reduce-scatter.4
where the time goes:
time: 624 us; the launch traced here: 618 us
  waiting for transfers between devices  375 us (60%)
  blocking collectives  127 us (20%)
  local copies, waits for them, and re-layouts  42.7 us (7%)
  matrix products  40.1 us (6%)
  other arithmetic  14.2 us (2%)
  between operations  13.7 us (2%)
    reduce_scatter x1, waiting for transfers between devices, on_device(): lax.psum_scatter(partial_value, 'row', scatter_dimension=3, tiled=True)  272 us
    all_to_all x1, blocking collectives, on_device(): lax.all_to_all(outgoing, 'col', split_axis=0, concat_axis=0, tiled=True)  127 us
    all_to_all x1, waiting for transfers between devices, on_device(): lax.all_to_all(summed, 'col', split_axis=0, concat_axis=0, tiled=True)  45.9 us
    all_gather x1, waiting for transfers between devices, on_device(): lax.all_gather(shared_down_weight, 'col', axis=1, tiled=True)  31.8 us
    all_gather x1, waiting for transfers between devices, on_device(): all_features = lax.all_gather(tokens, 'row', axis=1, tiled=True)  22.8 us
    gather x1, local copies, waits for them, and re-layouts, on_device(): jnp.take(all_features, jnp.minimum(slot_token, token_count - 1), axis=0)  17.7 us
    dot_general x1, matrix products, on_device(): jnp.einsum('sexf,efd->sexd', hidden, routed_down_weight, preferred_elemen...  14.2 us
  transfers between devices with their start and end apart: 8, of which 4 were waited for; matrix products, arithmetic and copies ran while one was open for 15% of the time, Pallas kernels for 0%

commit v1 on v0

v1 whole, which is shorter than its diff:
```python
import jax
import jax.numpy as jnp
from jax import lax
from jax.sharding import PartitionSpec as P

ADAPTER_SCALE = 2.0
BF = jnp.bfloat16
F32 = jnp.float32


def dot(a, b):
    return jnp.dot(a, b, preferred_element_type=F32)


def on_device(
    tokens,
    router,
    shared_gate_vector,
    shared_gate_weight,
    shared_up_weight,
    shared_down_weight,
    routed_gate_weight,
    routed_up_weight,
    routed_down_weight,
    adapter_input_factor,
    adapter_output_factor,
    routes,
    lengths,
    prompt_adapter_index,
    active_adapter_index,
):
    token_count, local_width = tokens.shape
    col_count = lax.axis_size("col")
    col = lax.axis_index("col")
    local_experts = routed_gate_weight.shape[0]
    expert_count = local_experts * col_count
    route_count = routes.shape[1]
    capacity = 2 * token_count * route_count // expert_count
    adapter_count, rank, _ = adapter_input_factor.shape
    request_count = lengths.shape[1]

    all_features = lax.all_gather(tokens, "row", axis=1, tiled=True)
    full_width = all_features.shape[1]
    all_routes = lax.all_gather(routes, "col", axis=0, tiled=False)
    all_tokens = lax.all_gather(all_features, "col", axis=0, tiled=False)
    gate_full = lax.all_gather(shared_gate_weight, "col", axis=0, tiled=True)
    up_full = lax.all_gather(shared_up_weight, "col", axis=0, tiled=True)
    down_full = lax.all_gather(shared_down_weight, "col", axis=1, tiled=True)

    steps = jnp.arange(request_count, dtype=jnp.int32)
    ends = jnp.sum(jnp.where(steps[:, None] <= steps[None, :], lengths[0][:, None], 0), axis=0)
    position = jnp.arange(token_count, dtype=jnp.int32)
    request_of = jnp.sum((position[:, None] >= ends[None, :]).astype(jnp.int32), axis=1)
    adapter_of_request = jnp.sum(
        jnp.where(
            prompt_adapter_index[0][:, None] == jnp.arange(active_adapter_index.shape[0])[None, :],
            active_adapter_index[None, :],
            0,
        ),
        axis=1,
    )
    adapter_of = jnp.sum(
        jnp.where(request_of[:, None] == steps[None, :], adapter_of_request[None, :], 0), axis=1
    )
    owner = jnp.arange(adapter_count * rank, dtype=jnp.int32) // rank
    mask = adapter_of[:, None] == owner[None, :]
    low_part = lax.dot_general(
        tokens,
        adapter_input_factor.reshape(adapter_count * rank, local_width),
        (((1,), (1,)), ((), ())),
        preferred_element_type=F32,
    )
    low_own = jnp.sum(
        jnp.where(mask, low_part, 0.0).reshape(token_count, adapter_count, rank), axis=1
    )
    low = lax.psum(low_own, "row").astype(BF)
    low_masked = jnp.where(mask, jnp.tile(low, (1, adapter_count)), jnp.zeros((), BF))
    delta = dot(
        low_masked, adapter_output_factor.reshape(adapter_count * rank, adapter_output_factor.shape[2])
    )

    logits = dot(all_features, router)
    experts = jnp.arange(expert_count, dtype=jnp.int32)
    onehot = routes[:, :, None] == experts[None, None, :]
    picked = jnp.sum(jnp.where(onehot, logits[:, None, :], 0.0), axis=2)
    raw_exp = jnp.exp(picked)
    gate_weights = raw_exp / jnp.sum(raw_exp, axis=1, keepdims=True)
    share = jax.nn.sigmoid(dot(all_features, shared_gate_vector))
    tri = (position[None, :] < position[:, None]).astype(BF)
    hit = jnp.any(onehot, axis=1)
    rank_own = dot(tri, hit.astype(BF)).astype(jnp.int32)
    weight_of = jnp.sum(jnp.where(onehot, gate_weights[:, :, None], 0.0), axis=1)
    slots = jnp.arange(capacity, dtype=jnp.int32)
    here = hit[:, :, None] & (rank_own[:, :, None] == slots[None, None, :])
    combine = jnp.where(here, weight_of[:, :, None], 0.0).reshape(token_count, expert_count * capacity)
    combine_hi = combine.astype(BF)
    combine_lo = (combine - combine_hi.astype(F32)).astype(BF)

    own_experts = col * local_experts + jnp.arange(local_experts, dtype=jnp.int32)
    hit_all = jnp.any(all_routes[:, :, :, None] == own_experts[None, None, None, :], axis=2)
    rank_all = jnp.einsum(
        "ts,gse->gte", tri, hit_all.astype(BF), preferred_element_type=F32
    ).astype(jnp.int32)
    pick = (
        (hit_all[:, :, :, None] & (rank_all[:, :, :, None] == slots[None, None, None, :]))
        .astype(BF)
        .transpose(2, 0, 3, 1)
    )
    rows = jnp.einsum("egst,gtd->egsd", pick, all_tokens, preferred_element_type=F32).astype(BF)
    rows = rows.reshape(local_experts, col_count * capacity, full_width)
    gate_part = jnp.einsum("esd,edf->esf", rows, routed_gate_weight, preferred_element_type=F32)
    up_part = jnp.einsum("esd,edf->esf", rows, routed_up_weight, preferred_element_type=F32)
    hidden = (jax.nn.silu(gate_part) * up_part).astype(BF)
    partial = jnp.einsum(
        "esf,efd->esd", hidden, routed_down_weight, preferred_element_type=F32
    ).astype(BF)
    outgoing = partial.reshape(local_experts, col_count, capacity, full_width).transpose(1, 0, 2, 3)
    returned = lax.all_to_all(outgoing, "col", split_axis=0, concat_axis=0, tiled=True)
    flat = returned.reshape(expert_count * capacity, full_width)

    shared_gate_value = dot(all_features, gate_full)
    shared_up_value = dot(all_features, up_full)
    shared_hidden = (
        jax.nn.silu(shared_gate_value) * (shared_up_value + ADAPTER_SCALE * delta)
    ).astype(BF)
    shared_part = dot(shared_hidden, down_full) * share[:, None]

    total = dot(combine_hi, flat) + dot(combine_lo, flat) + shared_part
    return lax.psum_scatter(total, "row", scatter_dimension=1, tiled=True)


def solution(mesh):
    return jax.shard_map(
        on_device,
        mesh=mesh,
        in_specs=(
            P("col", "row"),
            P(),
            P(),
            P("col", "row"),
            P("col", "row"),
            P("row", "col"),
            P("col", None, "row"),
            P("col", None, "row"),
            P("col", "row", None),
            P(None, None, "row"),
            P(None, None, "row"),
            P("col", None),
            P("col", None),
            P("col", None),
            P(),
        ),
        out_specs=P("col", "row"),
        check_vma=False,
    )
```

time: 624 us -> 373 us (0.60)
  waiting for transfers between devices: 375 us -> 238 us
  blocking collectives: 127 us -> 21.9 us
  local copies, waits for them, and re-layouts: 42.7 us -> 18 us
  matrix products: 40.1 us -> 64.7 us
  other arithmetic: 14.2 us -> 6.99 us
    reduce_scatter x2 -> x1, waiting for transfers between devices: 272 us -> 41.2 us  [on_device(): return lax.psum_scatter(total, 'row', scatter_dimension=1, tiled=True)]
    all_gather x4, waiting for transfers between devices: 31.8 us -> 164 us  [the longest x1 74 us: on_device(): down_full = lax.all_gather(shared_down_weight, 'col', axis=1, tiled=True)]
    all_to_all x1 -> x0, blocking collectives: 127 us -> none  [on_device(): lax.all_to_all(outgoing, 'col', split_axis=0, concat_axis=0, tiled=True)]
    all_to_all x1, waiting for transfers between devices: 45.9 us -> 0.01 us  [on_device(): lax.all_to_all(outgoing, 'col', split_axis=0, concat_axis=0, tiled=True)]
    gather x5 -> x0, local copies, waits for them, and re-layouts: 32.6 us -> none  [the longest x1 17.7 us: on_device(): jnp.take(all_features, jnp.minimum(slot_token, token_count - 1), axis=0)]
    dot_general x8 -> x13, matrix products: 40.1 us -> 64.7 us  [the longest x8 33.7 us: dot(): return jnp.dot(a, b, preferred_element_type=F32)]
    psum x0 -> x1, blocking collectives: none -> 12.1 us  [on_device(): low = lax.psum(low_own, 'row').astype(BF)]
    all_gather x0 -> x1, blocking collectives: none -> 9.74 us  [on_device(): all_routes = lax.all_gather(routes, 'col', axis=0, tiled=False)]
  transfers between devices with their start and end apart: 8 -> 7, of which waited for: 4 -> 5; matrix products, arithmetic and copies ran while one was open for 15% -> 21% of each run, Pallas kernels for 0% -> 0%
where the time goes in v1:
time: 373 us; the launch traced here: 369 us
  waiting for transfers between devices  238 us (64%)
  matrix products  64.7 us (17%)
  blocking collectives  21.9 us (6%)
  local copies, waits for them, and re-layouts  18 us (5%)
  between operations  13.7 us (4%)
  other arithmetic  6.99 us (2%)
  starting transfers between devices  5.81 us (2%)
    all_gather x1, waiting for transfers between devices, on_device(): down_full = lax.all_gather(shared_down_weight, 'col', axis=1, tiled=True)  74 us
    all_gather x1, waiting for transfers between devices, on_device(): up_full = lax.all_gather(shared_up_weight, 'col', axis=0, tiled=True)  45.1 us
    all_gather x1, waiting for transfers between devices, on_device(): all_tokens = lax.all_gather(all_features, 'col', axis=0, tiled=False)  44.5 us
    reduce_scatter x1, waiting for transfers between devices, on_device(): return lax.psum_scatter(total, 'row', scatter_dimension=1, tiled=True)  41.2 us
    dot_general x8, matrix products, dot(): return jnp.dot(a, b, preferred_element_type=F32)  33.7 us
    all_gather x1, waiting for transfers between devices, on_device(): all_features = lax.all_gather(tokens, 'row', axis=1, tiled=True)  30.5 us
    dot_general x1, matrix products, on_device(): jnp.einsum('esf,efd->esd', hidden, routed_down_weight, preferred_element_...  13.3 us
    psum x1, blocking collectives, on_device(): low = lax.psum(low_own, 'row').astype(BF)  12.1 us
  transfers between devices with their start and end apart: 7, of which 5 were waited for; matrix products, arithmetic and copies ran while one was open for 21% of the time, Pallas kernels for 0%

profile of v1, /device:TPU:11, one launch (start us, length us, event | category | flops | bytes accessed | tf_op | source)
XLA Modules:
  0.0 368.8 jit_solution(1594255409065002384)
XLA Ops:
  6.5 0.0 copy-start
  6.5 0.0 all-gather.8.cloned.1.call-start
  6.5 0.7 all-gather.8.cloned.1.call-update
  7.3 0.0 all-gather.16.cloned.1.call-start
  7.3 30.5 %all-gather.8.cloned.1.call-done = bf16[256,2048]{1,0:T(8,128)(2,1)} async-done(((bf16[256,512]{1,0:T(8,128)(2,1)}), bf16[256,2048]{1,0:T(8,128)(2,1)}) %all-gather.8.cloned.1.call-update) | async-done | bytes 1048592 | tf_op jit(solution)/shard_map/all_gather | solution.py:42
  37.8 0.0 all-gather.16.cloned.1.call-update
  37.8 0.0 all-gather.10.cloned.1.call-start
  37.8 0.7 all-gather.10.cloned.1.call-update
  38.5 0.0 all-gather.14.cloned.1.call-start
  38.6 0.5 all-gather.14.cloned.1.call-update
  39.1 0.0 all-gather.12.cloned.1.call-start
  39.2 0.5 all-gather.12.cloned.1.call-update
  39.7 0.0 copy-done.7
  39.7 9.7 %all-gather = s32[2048,4]{0,1:T(4,128)S(1)} all-gather(s32[256,4]{0,1:T(4,128)S(1)} %copy-done.7), channel_id=2, replica_groups=mesh['row'=4,'col'=8] {'col'}, dimensions={0}, use_global_device_ids=true | all-gather | bytes 36864 | tf_op jit(solution)/shard_map/all_gather | solution.py:44
  49.5 0.1 compare_reduce_fusion
  49.6 0.2 fusion.8
  49.8 44.5 %all-gather.16.cloned.1.call-done = bf16[2048,2048]{1,0:T(8,128)(2,1)} async-done(((bf16[256,2048]{1,0:T(8,128)(2,1)}), bf16[2048,2048]{1,0:T(8,128)(2,1)}) %all-gather.16.cloned.1.call-update) | async-done | bytes 8388624 | tf_op jit(solution)/shard_map/all_gather | solution.py:45
  94.3 8.9 %convert_bitcast_fusion = bf16[2,8,128,2048]{3,2,0,1:T(8,128)(2,1)} fusion(bf16[8,256,2048,1]{2,1,3,0:T(8,128)(2,1)} %bitcast.65, s32[2,8,256]{2,0,1:T(2,128)S(1)} %copy.40, pred[2,8,256]{2,0,1:T(4,128)(4,1)S(1)} %copy.39), kind=kOutput, calls=%fused_computation.1 | convolution fusion | flops 2152726528 | bytes 16797696 | tf_op jit(solution)/shard_map/egst,gtd->egsd/dot_general | solution.py:109
  103.2 8.8 %copy.41 = bf16[2,8,128,2048]{3,2,1,0:T(8,128)(2,1)} copy(bf16[2,8,128,2048]{3,2,0,1:T(8,128)(2,1)} %convert_bitcast_fusion) | data formatting | bytes 16777216 | tf_op jit(solution)/shard_map/convert_element_type | solution.py:109
  112.0 0.0 copy-done.9
  112.0 8.2 %fusion.31 = f32[2,1024,352]{1,2,0:T(8,128)} fusion(bf16[2,1024,2048]{2,1,0:T(8,128)(2,1)} %bitcast.66, bf16[2,2048,352]{1,2,0:T(8,128)(2,1)S(1)} %copy-done.9), kind=kOutput, calls=%fused_computation.71 | convolution fusion | flops 2952790016 | bytes 14155776 | tf_op jit(solution)/shard_map/esd,edf->esf/dot_general | solution.py:111
  120.3 0.0 copy-done
  120.3 13.3 %convolution_convert_fusion = bf16[2,1024,2048]{2,1,0:T(8,128)(2,1)} fusion(bf16[2,352,2048]{2,1,0:T(8,128)(2,1)S(1)} %copy-done, f32[2,1024,352]{1,2,0:T(8,128)} %fusion.31, bf16[2,1024,2048]{2,1,0:T(8,128)(2,1)} %bitcast.67, bf16[2,2048,352]{1,2,0:T(8,128)(2,1)} %param.22), kind=kOutput, calls=%fused_computation.2 | convolution fusion | flops 5914099712 | bytes 25427968 | tf_op jit(solution)/shard_map/esf,efd->esd/dot_general | solution.py:114
  133.5 8.4 %copy.58 = bf16[2,8,128,2048]{3,2,0,1:T(8,128)(2,1)} copy(bf16[2,8,128,2048]{3,2,1,0:T(8,128)(2,1)} %bitcast.68) | data formatting | bytes 16777216 | tf_op jit(solution)/shard_map/reshape | solution.py:117
  141.9 0.0 copy-start.3
  141.9 0.0 copy-start.4
  141.9 5.7 %all-to-all-start = ((bf16[8,2,128,2048]{3,2,1,0:T(8,128)(2,1)}), bf16[8,2,128,2048]{3,2,1,0:T(8,128)(2,1)}, u32[]{:S(2)}, u32[]{:S(2)}) async-start(bf16[8,2,128,2048]{3,2,1,0:T(8,128)(2,1)} %bitcast.64), calls=%async_computation | async-start | bytes 16777216 | tf_op jit(solution)/shard_map/all_to_all | solution.py:118
  147.6 0.0 reduce-scatter.2.cloned.1.call-start
  147.6 0.0 copy-done.8
  147.6 0.0 copy-done.10
  147.6 0.1 select_reduce_fusion.4
  147.7 0.1 convert_reduce_fusion
  147.8 0.0 copy-done.11
  147.8 0.0 copy-done.12
  147.8 0.2 select_reduce_fusion.3
  148.0 0.1 select_reduce_fusion.2
  148.1 0.0 copy-done.3
  148.1 0.0 copy-done.4
  148.1 0.5 convolution_select_fusion
  148.6 0.3 copy.43
  148.9 0.1 copy.36
  149.0 0.2 convolution_convert_fusion.2
  149.2 0.1 copy.37
  149.3 0.1 reduce_sum.79
  149.4 12.1 %psum.7 = bf16[256,16]{0,1:T(8,128)(2,1)S(1)} all-reduce(f32[256,16]{0,1:T(8,128)S(1)} %reduce_sum.79), channel_id=1, replica_groups=mesh['row'=4,'col'=8] {'row'}, use_global_device_ids=true, to_apply=%region_10.11 | all-reduce | flops 4096 | bytes 24576 | tf_op jit(solution)/shard_map/psum | solution.py:76
  161.6 0.0 copy-start.2
  161.6 0.0 copy-start.6
  161.6 4.1 %fusion = f32[256,1408]{1,0:T(8,128)} fusion(bf16[64,16,1408]{2,1,0:T(8,128)(2,1)} %param.25, s32[64,16]{1,0:T(8,128)S(1)} %add_select_fusion, s32[256]{0:T(256)S(1)} %select_reduce_fusion.2, bf16[256,16]{0,1:T(8,128)(2,1)S(1)} %psum.7), kind=kOutput, calls=%fused_computation.8 | convolution fusion | flops 739082240 | bytes 4338688 | tf_op jit(solution)/shard_map/dot_general | solution.py:12
  165.7 0.0 copy-done.6
  165.7 0.4 fusion.30
  166.2 0.1 copy.38
  166.3 0.4 fusion.33
  166.7 2.2 select_convert_fusion
  168.9 4.0 %fusion.4 = bf16[256,16,128]{2,1,0:T(8,128)(2,1)} fusion(f32[256,16]{1,0:T(8,128)S(1)} %copy.38, s32[256,16]{1,0:T(8,128)S(1)} %copy.37, pred[256,16]{1,0:T(8,128)(4,1)S(1)} %copy.36), kind=kLoop, calls=%fused_computation.14 | loop fusion | flops 3670016 | bytes 1085440 | tf_op jit(solution)/shard_map/convert_element_type | solution.py:97
  172.9 5.5 %fusion.32 = f32[256,1408]{1,0:T(8,128)} fusion(bf16[256,2048]{1,0:T(8,128)(2,1)S(1)} %copy-done.2, bf16[2048,1408]{1,0:T(8,128)(2,1)} %all-gather.10.cloned.1.call-done), kind=kOutput, calls=%fused_computation.72 | convolution fusion | flops 1476395008 | bytes 8257536 | tf_op jit(solution)/shard_map/dot_general | solution.py:12
  178.5 74.0 %all-gather.14.cloned.1.call-done = bf16[1408,2048]{1,0:T(8,128)(2,1)} async-done(((bf16[1408,256]{1,0:T(8,128)(2,1)}), bf16[1408,2048]{1,0:T(8,128)(2,1)}) %all-gather.14.cloned.1.call-update) | async-done | bytes 5767184 | tf_op jit(solution)/shard_map/all_gather | solution.py:48
  252.4 45.1 %all-gather.12.cloned.1.call-done = bf16[2048,1408]{1,0:T(8,128)(2,1)} async-done(((bf16[256,1408]{1,0:T(8,128)(2,1)}), bf16[2048,1408]{1,0:T(8,128)(2,1)}) %all-gather.12.cloned.1.call-update) | async-done | bytes 5767184 | tf_op jit(solution)/shard_map/all_gather | solution.py:47
  297.5 10.0 %convolution_multiply_fusion = f32[256,2048]{1,0:T(8,128)} fusion(bf16[1408,2048]{1,0:T(8,128)(2,1)} %all-gather.14.cloned.1.call-done, f32[256]{0:T(256)S(1)} %add_divide_fusion, f32[256,1408]{1,0:T(8,128)} %fusion, bf16[256,2048]{1,0:T(8,128)(2,1)S(1)} %copy-done.2, bf16[2048,1408]{1,0:T(8,128)(2,1)} %all-gather.12.cloned.1.call-done, f32[256,1408]{1,0:T(8,128)} %fusion.32), kind=kOutput, calls=%fused_computation.6 | convolution fusion | flops 2955837440 | bytes 17564672 | tf_op jit(solution)/shard_map/dot_general | solution.py:12
  307.5 0.0 all-to-all-done
  307.5 5.9 %fusion.11 = f32[256,2048]{1,0:T(8,128)S(1)} fusion(bf16[2048,2048]{1,0:T(8,128)(2,1)} %bitcast.10, bf16[32,8,16,128]{3,2,1,0:T(8,128)(2,1)S(1)} %bitcast.72), kind=kOutput, calls=%fused_computation.25 | convolution fusion | flops 2147483648 | bytes 11534336 | tf_op jit(solution)/shard_map/dot_general | solution.py:12
  313.4 0.0 copy-start.1
  313.4 7.3 %fusion.2 = f32[256,2048]{1,0:T(8,128)} fusion(f32[256,2048]{1,0:T(8,128)S(1)} %copy-done.13, f32[256,2048]{1,0:T(8,128)S(1)} %fusion.11, bf16[2048,2048]{1,0:T(8,128)(2,1)} %bitcast.10, bf16[32,8,16,128]{3,2,1,0:T(8,128)(2,1)S(1)} %bitcast.71), kind=kOutput, calls=%fused_computation.12 | convolution fusion | flops 2148532224 | bytes 15728640 | tf_op jit(solution)/shard_map/dot_general | solution.py:12
  320.7 0.0 reduce-scatter.2.cloned.1.call-update
  320.8 41.2 %reduce-scatter.2.cloned.1.call-done = f32[256,512]{1,0:T(8,128)} async-done(((f32[256,2048]{1,0:T(8,128)}), f32[256,512]{1,0:T(8,128)}) %reduce-scatter.2.cloned.1.call-update) | async-done | bytes 524304 | tf_op jit(solution)/shard_map/reduce_scatter | solution.py:129
  (26 shorter events, 0.2 us)
Async XLA Ops:
  6.5 113.7 %copy-start = (bf16[2,352,2048]{2,1,0:T(8,128)(2,1)S(1)}, bf16[2,352,2048]{2,1,0:T(8,128)(2,1)}, u32[]{:S(2)}) copy-start(bf16[2,352,2048]{2,1,0:T(8,128)(2,1)} %param.23) | copy-start | bytes 8650756
  6.5 33.2 %copy-start.7 = (s32[256,4]{0,1:T(4,128)S(1)}, s32[256,4]{0,1:T(4,128)}, u32[]{:S(2)}) copy-start(s32[256,4]{0,1:T(4,128)} %param.26) | copy-start | bytes 12292
  6.5 31.2 %all-gather.8.cloned.1.call-start = ((), (), s32[]{:S(2)}) async-start(), calls=%async_computation.2 | async-start | bytes 1310720 | tf_op jit(solution)/shard_map/all_gather | solution.py:42
  7.3 87.0 %all-gather.16.cloned.1.call-start = ((), (), s32[]{:S(2)}) async-start(), calls=%async_computation.7 | async-start | bytes 9437184 | tf_op jit(solution)/shard_map/all_gather | solution.py:45
  37.8 135.1 %all-gather.10.cloned.1.call-start = ((), (), s32[]{:S(2)}) async-start(), calls=%async_computation.3 | async-start | bytes 6488064 | tf_op jit(solution)/shard_map/all_gather | solution.py:46
  38.5 213.9 %all-gather.14.cloned.1.call-start = ((), (), s32[]{:S(2)}) async-start(), calls=%async_computation.5 | async-start | bytes 6488064 | tf_op jit(solution)/shard_map/all_gather | solution.py:48
  39.1 258.4 %all-gather.12.cloned.1.call-start = ((), (), s32[]{:S(2)}) async-start(), calls=%async_computation.4 | async-start | bytes 6488064 | tf_op jit(solution)/shard_map/all_gather | solution.py:47
  103.2 8.8 %copy-start.9 = (bf16[2,2048,352]{1,2,0:T(8,128)(2,1)S(1)}, bf16[2,2048,352]{1,2,0:T(8,128)(2,1)}, u32[]{:S(2)}) copy-start(bf16[2,2048,352]{1,2,0:T(8,128)(2,1)} %param.21) | copy-start | bytes 8650756
  141.9 5.7 %copy-start.8 = (bf16[2048]{0:T(1024)(128)(2,1)S(1)}, bf16[2048]{0:T(1024)(128)(2,1)}, u32[]{:S(2)}) copy-start(bf16[2048]{0:T(1024)(128)(2,1)} %param.17) | copy-start | bytes 12292
  141.9 5.7 %copy-start.10 = (s32[1,16]{1,0:T(1,128)S(1)}, s32[1,16]{1,0:T(1,128)}, u32[]{:S(2)}) copy-start(s32[1,16]{1,0:T(1,128)} %param.27) | copy-start | bytes 196
  141.9 5.9 %copy-start.11 = (s32[16]{0:T(128)S(1)}, s32[16]{0:T(128)}, u32[]{:S(2)}) copy-start(s32[16]{0:T(128)} %param.29) | copy-start | bytes 196
  141.9 5.9 %copy-start.12 = (s32[1,16]{1,0:T(1,128)S(1)}, s32[1,16]{1,0:T(1,128)}, u32[]{:S(2)}) copy-start(s32[1,16]{1,0:T(1,128)} %param.28) | copy-start | bytes 196
  141.9 6.2 %copy-start.3 = (bf16[256,512]{1,0:T(8,128)(2,1)S(1)}, bf16[256,512]{1,0:T(8,128)(2,1)}, u32[]{:S(2)}) copy-start(bf16[256,512]{1,0:T(8,128)(2,1)} %param.15) | copy-start | bytes 786436
  141.9 6.2 %copy-start.4 = (bf16[64,16,512]{2,1,0:T(8,128)(2,1)S(1)}, bf16[64,16,512]{2,1,0:T(8,128)(2,1)}, u32[]{:S(2)}) copy-start(bf16[64,16,512]{2,1,0:T(8,128)(2,1)} %param.24) | copy-start | bytes 3145732
  141.9 165.6 %all-to-all-start = ((bf16[8,2,128,2048]{3,2,1,0:T(8,128)(2,1)}), bf16[8,2,128,2048]{3,2,1,0:T(8,128)(2,1)}, u32[]{:S(2)}, u32[]{:S(2)}) async-start(bf16[8,2,128,2048]{3,2,1,0:T(8,128)(2,1)} %bitcast.64), calls=%async_computation | async-start | bytes 16777216 | tf_op jit(solution)/shard_map/all_to_all | solution.py:118
  147.6 214.4 %reduce-scatter.2.cloned.1.call-start = ((), (), s32[]{:S(2)}) async-start(), calls=%async_computation.6 | async-start | bytes 2621440 | tf_op jit(solution)/shard_map/reduce_scatter | solution.py:129
  161.6 4.1 %copy-start.2 = (bf16[256,2048]{1,0:T(8,128)(2,1)S(1)}, bf16[256,2048]{1,0:T(8,128)(2,1)}, u32[]{:S(2)}) copy-start(bf16[256,2048]{1,0:T(8,128)(2,1)} %all-gather.8.cloned.1.call-done) | copy-start | bytes 3145732
  161.6 4.1 %copy-start.6 = (bf16[2048,16]{0,1:T(8,128)(2,1)S(1)}, bf16[2048,16]{0,1:T(8,128)(2,1)}, u32[]{:S(2)}) copy-start(bf16[2048,16]{0,1:T(8,128)(2,1)} %param.16) | copy-start | bytes 196612
  307.5 5.9 %copy-start.5 = (bf16[256,16,128]{2,1,0:T(8,128)(2,1)S(1)}, bf16[256,16,128]{2,1,0:T(8,128)(2,1)}, u32[]{:S(2)}) copy-start(bf16[256,16,128]{2,1,0:T(8,128)(2,1)} %fusion.4) | copy-start | bytes 3145732
  307.5 5.9 %copy-start.13 = (f32[256,2048]{1,0:T(8,128)S(1)}, f32[256,2048]{1,0:T(8,128)}, u32[]{:S(2)}) copy-start(f32[256,2048]{1,0:T(8,128)} %convolution_multiply_fusion) | copy-start | bytes 6291460
  313.4 48.5 %copy-start.1 = (bf16[2,352,2048]{2,1,0:T(8,128)(2,1)S(1)}, bf16[2,352,2048]{2,1,0:T(8,128)(2,1)}, u32[]{:S(2)}) copy-start(bf16[2,352,2048]{2,1,0:T(8,128)(2,1)} %param.23) | copy-start | bytes 8650756
Sparse Core Ops, SparseCore 0:
  8.9 28.8 all-gather.7
  39.7 54.5 all-gather.15
  96.2 43.3 all-gather.9
  141.2 111.1 all-gather.13
  254.2 43.3 all-gather.11
  320.9 41.0 reduce-scatter.1

commit v2 on v1

--- a/solution.py
+++ b/solution.py
@@ -1,6 +1,10 @@
+import functools
+
 import jax
 import jax.numpy as jnp
 from jax import lax
+from jax.experimental import pallas as pl
+from jax.experimental.pallas import tpu as pltpu
 from jax.sharding import PartitionSpec as P
 
 ADAPTER_SCALE = 2.0
@@ -10,6 +14,137 @@
 
 def dot(a, b):
     return jnp.dot(a, b, preferred_element_type=F32)
+
+
+def remote(src, dst, send, recv, row, col):
+    return pltpu.make_async_remote_copy(
+        src_ref=src,
+        dst_ref=dst,
+        send_sem=send,
+        recv_sem=recv,
+        device_id=(row, col),
+        device_id_type=pl.DeviceIdType.MESH,
+    )
+
+
+def greet(nrow, ncol, row, col):
+    barrier = pltpu.get_barrier_semaphore()
+    for k in range(1, nrow):
+        pl.semaphore_signal(
+            barrier,
+            inc=1,
+            device_id=(lax.rem(row + k, nrow), col),
+            device_id_type=pl.DeviceIdType.MESH,
+        )
+    for k in range(1, ncol):
+        pl.semaphore_signal(
+            barrier,
+            inc=1,
+            device_id=(row, lax.rem(col + k, ncol)),
+            device_id_type=pl.DeviceIdType.MESH,
+        )
+    pl.semaphore_wait(barrier, nrow + ncol - 2)
+
+
+def gather_kernel(
+    nrow, ncol, tok, rts, low, out, rts_out, low_out,
+    own_sem, z_send, z_recv, g_send, g_recv, pair_send, pass_send, r_send, r_recv, l_send, l_recv,
+):
+    row, col = lax.axis_index("row"), lax.axis_index("col")
+    pair = col + 1 - 2 * lax.rem(col, 2)
+    width = tok.shape[1]
+    half = ncol // 2
+
+    def block(group, part):
+        return out.at[group, :, pl.ds(pl.multiple_of(part * width, width), width)]
+
+    greet(nrow, ncol, row, col)
+    own = [
+        pltpu.make_async_copy(tok, block(col, row), own_sem.at[0]),
+        pltpu.make_async_copy(rts, rts_out.at[col], own_sem.at[1]),
+        pltpu.make_async_copy(low, low_out.at[row], own_sem.at[2]),
+    ]
+    sent = []
+
+    def go(copy):
+        copy.start()
+        sent.append(copy)
+
+    for k in range(1, nrow):
+        there = lax.rem(row + k, nrow)
+        go(remote(tok, block(col, row), z_send.at[k], z_recv.at[row], there, col))
+    for k in range(nrow):
+        part = lax.rem(row + k, nrow)
+        if k:
+            remote(
+                block(col, part), block(col, part), z_send.at[k], z_recv.at[part], row, pair
+            ).wait_recv()
+        src = tok if k == 0 else block(col, part)
+        for m in range(1, half):
+            there = lax.rem(col + 2 * m, ncol)
+            go(remote(src, block(col, part), g_send.at[k, m], g_recv.at[col, part], row, there))
+        go(remote(src, block(col, part), pair_send.at[k], g_recv.at[col, part], row, pair))
+        if k == 0:
+            for copy in own:
+                copy.start()
+            for j in range(1, nrow):
+                there = lax.rem(row + j, nrow)
+                go(remote(low, low_out.at[row], l_send.at[j], l_recv.at[row], there, col))
+            for j in range(1, ncol):
+                there = lax.rem(col + j, ncol)
+                go(remote(rts, rts_out.at[col], r_send.at[j], r_recv.at[col], row, there))
+    for k in range(nrow):
+        part = lax.rem(row + k, nrow)
+        for m in range(1, half):
+            group = lax.rem(col + ncol - 2 * m, ncol)
+            copy = remote(
+                block(group, part), block(group, part), pass_send.at[k, m], g_recv.at[group, part], row, pair
+            )
+            copy.wait_recv()
+            go(copy)
+    for k in range(nrow):
+        part = lax.rem(row + k, nrow)
+        for m in range(half):
+            group = lax.rem(pair + ncol - 2 * m, ncol)
+            remote(
+                block(group, part), block(group, part), pass_send.at[k, m], g_recv.at[group, part], row, pair
+            ).wait_recv()
+    for j in range(1, nrow):
+        there = lax.rem(row + j, nrow)
+        remote(low, low_out.at[there], l_send.at[j], l_recv.at[there], there, col).wait_recv()
+    for j in range(1, ncol):
+        there = lax.rem(col + j, ncol)
+        remote(rts, rts_out.at[there], r_send.at[j], r_recv.at[there], row, there).wait_recv()
+    for copy in own:
+        copy.wait()
+    for copy in sent:
+        copy.wait_send()
+
+
+def gather_tokens(tokens, routes_t, low_t):
+    nrow, ncol = lax.axis_size("row"), lax.axis_size("col")
+    count, width = tokens.shape
+    half = ncol // 2
+    dma = pltpu.SemaphoreType.DMA
+    return pl.pallas_call(
+        functools.partial(gather_kernel, nrow, ncol),
+        out_shape=(
+            jax.ShapeDtypeStruct((ncol, count, nrow * width), tokens.dtype),
+            jax.ShapeDtypeStruct((ncol, *routes_t.shape), routes_t.dtype),
+            jax.ShapeDtypeStruct((nrow, *low_t.shape), low_t.dtype),
+        ),
+        in_specs=[pl.BlockSpec(memory_space=pl.ANY)] * 3,
+        out_specs=(pl.BlockSpec(memory_space=pl.ANY),) * 3,
+        scratch_shapes=[
+            dma((3,)), dma((nrow,)), dma((nrow,)), dma((nrow, half)), dma((ncol, nrow)), dma((nrow,)),
+            dma((nrow, half)), dma((ncol,)), dma((ncol,)), dma((nrow,)), dma((nrow,)),
+        ],
+        compiler_params=pltpu.CompilerParams(collective_id=0, has_side_effects=True),
+        cost_estimate=pl.CostEstimate(
+            flops=0, bytes_accessed=20 * ncol * count * width * nrow, transcendentals=0
+        ),
+        name="gather_tokens",
+    )(tokens, routes_t, low_t)
 
 
 def on_device(
@@ -39,10 +174,6 @@
     adapter_count, rank, _ = adapter_input_factor.shape
     request_count = lengths.shape[1]
 
-    all_features = lax.all_gather(tokens, "row", axis=1, tiled=True)
-    full_width = all_features.shape[1]
-    all_routes = lax.all_gather(routes, "col", axis=0, tiled=False)
-    all_tokens = lax.all_gather(all_features, "col", axis=0, tiled=False)
     gate_full = lax.all_gather(shared_gate_weight, "col", axis=0, tiled=True)
     up_full = lax.all_gather(shared_up_weight, "col", axis=0, tiled=True)
     down_full = lax.all_gather(shared_down_weight, "col", axis=1, tiled=True)
@@ -73,7 +204,11 @@
     low_own = jnp.sum(
         jnp.where(mask, low_part, 0.0).reshape(token_count, adapter_count, rank), axis=1
     )
-    low = lax.psum(low_own, "row").astype(BF)
+    routes_t = jnp.pad(routes.T, ((0, 8 - route_count), (0, 0)), constant_values=-1)
+    all_tokens, all_routes_t, low_all = gather_tokens(tokens, routes_t, low_own.T)
+    all_features = lax.dynamic_index_in_dim(all_tokens, col, 0, keepdims=False)
+    full_width = all_features.shape[1]
+    low = jnp.sum(low_all, axis=0).T.astype(BF)
     low_masked = jnp.where(mask, jnp.tile(low, (1, adapter_count)), jnp.zeros((), BF))
     delta = dot(
         low_masked, adapter_output_factor.reshape(adapter_count * rank, adapter_output_factor.shape[2])
@@ -97,7 +232,7 @@
     combine_lo = (combine - combine_hi.astype(F32)).astype(BF)
 
     own_experts = col * local_experts + jnp.arange(local_experts, dtype=jnp.int32)
-    hit_all = jnp.any(all_routes[:, :, :, None] == own_experts[None, None, None, :], axis=2)
+    hit_all = jnp.any(all_routes_t[:, :, :, None] == own_experts[None, None, None, :], axis=1)
     rank_all = jnp.einsum(
         "ts,gse->gte", tri, hit_all.astype(BF), preferred_element_type=F32
     ).astype(jnp.int32)

time: 373 us -> 347 us (0.930)
  waiting for transfers between devices: 238 us -> 139 us
  Pallas kernels: 0 us -> 82.1 us
  blocking collectives: 21.9 us -> 0 us
  matrix products: 64.7 us -> 70.4 us
  other arithmetic: 6.99 us -> 11.3 us
    all_to_all x1, waiting for transfers between devices: 0.01 us -> 97.5 us  [on_device(): lax.all_to_all(outgoing, 'col', split_axis=0, concat_axis=0, tiled=True)]
    pallas_call x0 -> x1, Pallas kernels: none -> 82.1 us  [gather_tokens(): pl.pallas_call(functools.partial(gather_kernel, nrow, ncol), out_shape=(j...]
    all_gather x2 -> x0, waiting for transfers between devices: 74.9 us -> none  [the longest x1 44.5 us: on_device(): all_tokens = lax.all_gather(all_features, 'col', axis=0, tiled=False)]
    all_gather x1, waiting for transfers between devices: 74 us -> 0.02 us  [on_device(): down_full = lax.all_gather(shared_down_weight, 'col', axis=1, tiled=True)]
    all_gather x1, waiting for transfers between devices: 45.1 us -> 0.02 us  [on_device(): up_full = lax.all_gather(shared_up_weight, 'col', axis=0, tiled=True)]
    psum x1 -> x0, blocking collectives: 12.1 us -> none  [on_device(): low = lax.psum(low_own, 'row').astype(BF)]
    all_gather x1 -> x0, blocking collectives: 9.74 us -> none  [on_device(): all_routes = lax.all_gather(routes, 'col', axis=0, tiled=False)]
  transfers between devices with their start and end apart: 7 -> 5, of which waited for: 5 -> 2; matrix products, arithmetic and copies ran while one was open for 21% -> 24% of each run, Pallas kernels for 0% -> 24%
where the time goes in v2:
time: 347 us; the launch traced here: 343 us
  waiting for transfers between devices  139 us (40%)
  Pallas kernels  82.1 us (24%)
  matrix products  70.4 us (20%)
  local copies, waits for them, and re-layouts  20.2 us (6%)
  between operations  13.3 us (4%)
  other arithmetic  11.3 us (3%)
  starting transfers between devices  5.89 us (2%)
    all_to_all x1, waiting for transfers between devices, on_device(): lax.all_to_all(outgoing, 'col', split_axis=0, concat_axis=0, tiled=True)  97.5 us
    pallas_call x1, Pallas kernels, gather_tokens(): pl.pallas_call(functools.partial(gather_kernel, nrow, ncol), out_shape=(j...  82.1 us
    reduce_scatter x1, waiting for transfers between devices, on_device(): return lax.psum_scatter(total, 'row', scatter_dimension=1, tiled=True)  39.6 us
    dot_general x8, matrix products, dot(): return jnp.dot(a, b, preferred_element_type=F32)  36.2 us
    dot_general x1, matrix products, on_device(): jnp.einsum('esf,efd->esd', hidden, routed_down_weight, preferred_element_...  12.9 us
    dot_general x1, matrix products, on_device(): jnp.einsum('egst,gtd->egsd', pick, all_tokens, preferred_element_type=F32)  9.23 us
    dot_general x1, matrix products, on_device(): jnp.einsum('esd,edf->esf', rows, routed_gate_weight, preferred_element_ty...  9.04 us
    convert_element_type x1, local copies, waits for them, and re-layouts, on_device(): jnp.einsum('egst,gtd->egsd', pick, all_tokens, preferred_element_type=F32)  8.4 us
  transfers between devices with their start and end apart: 5, of which 2 were waited for; matrix products, arithmetic and copies ran while one was open for 24% of the time, Pallas kernels for 24%

profile of v2, /device:TPU:11, one launch (start us, length us, event | category | flops | bytes accessed | tf_op | source)
XLA Modules:
  0.0 342.5 jit_solution(17234887700863352952)
XLA Ops:
  6.5 0.0 copy-start
  6.5 0.0 all-gather.4.cloned.1.call-start
  6.5 0.7 all-gather.4.cloned.1.call-update
  7.3 0.0 copy-start.4
  7.3 0.0 all-gather.6.cloned.1.call-start
  7.3 0.7 all-gather.6.cloned.1.call-update
  8.0 0.0 all-gather.8.cloned.1.call-start
  8.1 0.7 all-gather.8.cloned.1.call-update
  8.8 0.7 select_reduce_fusion.4
  9.5 0.1 convert_reduce_fusion
  9.6 0.9 select_reduce_fusion.3
  10.5 0.1 select_reduce_fusion.2
  10.6 2.8 convolution_select_fusion
  13.4 2.5 copy.35
  15.9 0.0 copy-done.4
  15.9 0.6 pad.4.rts
  16.5 2.0 reduce_sum.85
  18.5 82.1 %gather_tokens.1 = (bf16[8,256,2048]{2,1,0:T(8,128)(2,1)}, s32[8,8,256]{2,1,0:T(8,128)}, f32[4,16,256]{2,1,0:T(8,128)}) custom-call(bf16[256,512]{1,0:T(8,128)(2,1)} %tok.1, s32[8,256]{1,0:T(8,128)} %pad.4.rts, f32[16,256]{1,0:T(8,128)} %bitcast.78), custom_call_target="tpu_custom_call" | custom-call | bytes 83886080 | tf_op jit(solution)/shard_map/gather_tokens/pallas_call | solution.py:129
  100.6 1.0 compare_reduce_fusion
  101.6 0.2 fusion.12
  101.8 9.2 %convert_bitcast_fusion = bf16[2,8,128,2048]{3,2,0,1:T(8,128)(2,1)} fusion(bf16[8,256,2048]{2,1,0:T(8,128)(2,1)} %get-tuple-element.8, s32[2,8,256]{2,0,1:T(2,128)S(1)} %copy.38, pred[2,8,256]{2,0,1:T(4,128)(4,1)S(1)} %bitcast.80), kind=kOutput, calls=%fused_computation.3 | convolution fusion | flops 2152726528 | bytes 16797696 | tf_op jit(solution)/shard_map/egst,gtd->egsd/dot_general | solution.py:244
  111.0 0.0 copy-start.6
  111.0 8.4 %copy.39 = bf16[2,8,128,2048]{3,2,1,0:T(8,128)(2,1)} copy(bf16[2,8,128,2048]{3,2,0,1:T(8,128)(2,1)} %convert_bitcast_fusion) | data formatting | bytes 16777216 | tf_op jit(solution)/shard_map/convert_element_type | solution.py:244
  119.4 0.0 copy-done.6
  119.4 9.0 %fusion.53 = f32[2,1024,352]{1,2,0:T(8,128)} fusion(bf16[2,1024,2048]{2,1,0:T(8,128)(2,1)} %bitcast.71, bf16[2,2048,352]{1,2,0:T(8,128)(2,1)S(1)} %copy-done.6), kind=kOutput, calls=%fused_computation.88 | convolution fusion | flops 2952790016 | bytes 14155776 | tf_op jit(solution)/shard_map/esd,edf->esf/dot_general | solution.py:246
  128.5 0.0 copy-done
  128.5 12.9 %convolution_convert_fusion = bf16[2,1024,2048]{2,1,0:T(8,128)(2,1)} fusion(bf16[2,352,2048]{2,1,0:T(8,128)(2,1)S(1)} %copy-done, f32[2,1024,352]{1,2,0:T(8,128)} %fusion.53, bf16[2,1024,2048]{2,1,0:T(8,128)(2,1)} %bitcast.72, bf16[2,2048,352]{1,2,0:T(8,128)(2,1)} %param.22), kind=kOutput, calls=%fused_computation.4 | convolution fusion | flops 5914099712 | bytes 25427968 | tf_op jit(solution)/shard_map/esf,efd->esd/dot_general | solution.py:249
  141.4 8.3 %copy.55 = bf16[2,8,128,2048]{3,2,0,1:T(8,128)(2,1)} copy(bf16[2,8,128,2048]{3,2,1,0:T(8,128)(2,1)} %bitcast.73) | data formatting | bytes 16777216 | tf_op jit(solution)/shard_map/reshape | solution.py:252
  149.7 0.0 copy-start.5
  149.7 0.0 copy-start.3
  149.7 0.0 copy-start.2
  149.7 5.8 %all-to-all-start = ((bf16[8,2,128,2048]{3,2,1,0:T(8,128)(2,1)}), bf16[8,2,128,2048]{3,2,1,0:T(8,128)(2,1)}, u32[]{:S(2)}, u32[]{:S(2)}) async-start(bf16[8,2,128,2048]{3,2,1,0:T(8,128)(2,1)} %bitcast.70), calls=%async_computation | async-start | bytes 16777216 | tf_op jit(solution)/shard_map/all_to_all | solution.py:253
  155.5 0.0 reduce-scatter.2.cloned.1.call-start
  155.5 0.0 copy-done.5
  155.5 0.1 copy.33
  155.7 0.2 convolution_convert_fusion.2
  155.8 0.1 copy.34
  156.0 0.0 copy-done.3
  156.0 0.0 copy-done.2
  156.0 1.6 fusion.23
  157.7 0.1 copy.36
  157.8 1.6 fusion.18
  159.4 4.2 %fusion.8 = bf16[256,16,128]{2,1,0:T(8,128)(2,1)} fusion(f32[256,16]{1,0:T(8,128)S(1)} %copy.36, s32[256,16]{1,0:T(8,128)S(1)} %copy.34, pred[256,16]{1,0:T(8,128)(4,1)S(1)} %copy.33), kind=kLoop, calls=%fused_computation.16 | loop fusion | flops 3670016 | bytes 1085440 | tf_op jit(solution)/shard_map/convert_element_type | solution.py:232
  163.7 2.2 select_convert_fusion
  165.9 2.9 fusion.4
  168.8 97.5 %all-to-all-done = bf16[8,2,128,2048]{3,2,1,0:T(8,128)(2,1)} async-done(((bf16[8,2,128,2048]{3,2,1,0:T(8,128)(2,1)}), bf16[8,2,128,2048]{3,2,1,0:T(8,128)(2,1)}, u32[]{:S(2)}, u32[]{:S(2)}) %all-to-all-start) | async-done | bytes 8388640 | tf_op jit(solution)/shard_map/all_to_all | solution.py:253
  266.3 7.1 %fusion.15 = f32[256,2048]{1,0:T(8,128)} fusion(bf16[2048,2048]{1,0:T(8,128)(2,1)} %bitcast.16, bf16[32,8,16,128]{3,2,1,0:T(8,128)(2,1)S(1)} %bitcast.77), kind=kOutput, calls=%fused_computation.27 | convolution fusion | flops 2147483648 | bytes 11534336 | tf_op jit(solution)/shard_map/dot_general | solution.py:16
  273.4 0.0 all-gather.4.cloned.1.call-done
  273.4 4.8 %fusion.21 = f32[256,1408]{1,0:T(8,128)S(1)} fusion(bf16[2048,1408]{1,0:T(8,128)(2,1)} %all-gather.4.cloned.1.call-done, bf16[8,256,2048]{2,1,0:T(8,128)(2,1)} %get-tuple-element.8, s32[]{:T(128)S(6)} %select_n.73), kind=kOutput, calls=%fused_computation.33 | convolution fusion | flops 1476395008 | bytes 8257540 | tf_op jit(solution)/shard_map/dot_general | solution.py:16
  278.2 0.0 all-gather.6.cloned.1.call-done
  278.2 0.0 all-gather.8.cloned.1.call-done
  278.2 9.4 %convolution_multiply_fusion = f32[256,2048]{1,0:T(8,128)} fusion(bf16[1408,2048]{1,0:T(8,128)(2,1)} %all-gather.8.cloned.1.call-done, f32[256]{0:T(256)S(1)} %add_divide_fusion, f32[256,1408]{1,0:T(8,128)S(1)} %fusion.4, bf16[2048,1408]{1,0:T(8,128)(2,1)} %all-gather.6.cloned.1.call-done, f32[256,1408]{1,0:T(8,128)S(1)} %fusion.21, ...), kind=kOutput, calls=%fused_computation.8 | convolution fusion | flops 2955837440 | bytes 17564676 | tf_op jit(solution)/shard_map/dot_general | solution.py:16
  287.7 0.0 copy-start.1
  287.7 8.7 %fusion.6 = f32[256,2048]{1,0:T(8,128)} fusion(f32[256,2048]{1,0:T(8,128)} %convolution_multiply_fusion, f32[256,2048]{1,0:T(8,128)} %fusion.15, bf16[2048,2048]{1,0:T(8,128)(2,1)} %bitcast.16, bf16[32,8,16,128]{3,2,1,0:T(8,128)(2,1)} %bitcast.76), kind=kOutput, calls=%fused_computation.14 | convolution fusion | flops 2148532224 | bytes 15728640 | tf_op jit(solution)/shard_map/dot_general | solution.py:16
  296.4 0.0 reduce-scatter.2.cloned.1.call-update
  296.4 39.6 %reduce-scatter.2.cloned.1.call-done = f32[256,512]{1,0:T(8,128)} async-done(((f32[256,2048]{1,0:T(8,128)}), f32[256,512]{1,0:T(8,128)}) %reduce-scatter.2.cloned.1.call-update) | async-done | bytes 524304 | tf_op jit(solution)/shard_map/reduce_scatter | solution.py:264
  336.0 0.0 copy-done.1
  (12 shorter events, 0.2 us)
Async XLA Ops:
  6.5 122.0 %copy-start = (bf16[2,352,2048]{2,1,0:T(8,128)(2,1)S(1)}, bf16[2,352,2048]{2,1,0:T(8,128)(2,1)}, u32[]{:S(2)}) copy-start(bf16[2,352,2048]{2,1,0:T(8,128)(2,1)} %param.23) | copy-start | bytes 8650756
  6.5 266.9 %all-gather.4.cloned.1.call-start = ((), (), s32[]{:S(2)}) async-start(), calls=%async_computation.2 | async-start | bytes 6488064 | tf_op jit(solution)/shard_map/all_gather | solution.py:177
  7.3 8.7 %copy-start.4 = (s32[256,4]{0,1:T(4,128)S(1)}, s32[256,4]{0,1:T(4,128)}, u32[]{:S(2)}) copy-start(s32[256,4]{0,1:T(4,128)} %param.26) | copy-start | bytes 12292
  7.3 270.9 %all-gather.6.cloned.1.call-start = ((), (), s32[]{:S(2)}) async-start(), calls=%async_computation.3 | async-start | bytes 6488064 | tf_op jit(solution)/shard_map/all_gather | solution.py:178
  8.0 270.2 %all-gather.8.cloned.1.call-start = ((), (), s32[]{:S(2)}) async-start(), calls=%async_computation.4 | async-start | bytes 6488064 | tf_op jit(solution)/shard_map/all_gather | solution.py:179
  111.0 8.4 %copy-start.6 = (bf16[2,2048,352]{1,2,0:T(8,128)(2,1)S(1)}, bf16[2,2048,352]{1,2,0:T(8,128)(2,1)}, u32[]{:S(2)}) copy-start(bf16[2,2048,352]{1,2,0:T(8,128)(2,1)} %param.21) | copy-start | bytes 8650756
  149.7 5.8 %copy-start.5 = (bf16[2048]{0:T(1024)(128)(2,1)S(1)}, bf16[2048]{0:T(1024)(128)(2,1)}, u32[]{:S(2)}) copy-start(bf16[2048]{0:T(1024)(128)(2,1)} %param.17) | copy-start | bytes 12292
  149.7 6.3 %copy-start.3 = (f32[4,16,256]{2,1,0:T(8,128)S(1)}, f32[4,16,256]{2,1,0:T(8,128)}, u32[]{:S(2)}) copy-start(f32[4,16,256]{2,1,0:T(8,128)} %get-tuple-element.10) | copy-start | bytes 196612
  149.7 6.3 %copy-start.2 = (bf16[2048,16]{0,1:T(8,128)(2,1)S(1)}, bf16[2048,16]{0,1:T(8,128)(2,1)}, u32[]{:S(2)}) copy-start(bf16[2048,16]{0,1:T(8,128)(2,1)} %param.16) | copy-start | bytes 196612
  149.7 116.6 %all-to-all-start = ((bf16[8,2,128,2048]{3,2,1,0:T(8,128)(2,1)}), bf16[8,2,128,2048]{3,2,1,0:T(8,128)(2,1)}, u32[]{:S(2)}, u32[]{:S(2)}) async-start(bf16[8,2,128,2048]{3,2,1,0:T(8,128)(2,1)} %bitcast.70), calls=%async_computation | async-start | bytes 16777216 | tf_op jit(solution)/shard_map/all_to_all | solution.py:253
  155.5 180.5 %reduce-scatter.2.cloned.1.call-start = ((), (), s32[]{:S(2)}) async-start(), calls=%async_computation.5 | async-start | bytes 2621440 | tf_op jit(solution)/shard_map/reduce_scatter | solution.py:264
  287.7 48.3 %copy-start.1 = (bf16[2,352,2048]{2,1,0:T(8,128)(2,1)S(1)}, bf16[2,352,2048]{2,1,0:T(8,128)(2,1)}, u32[]{:S(2)}) copy-start(bf16[2,352,2048]{2,1,0:T(8,128)(2,1)} %param.23) | copy-start | bytes 8650756
Sparse Core Ops, SparseCore 0:
  9.2 83.3 all-gather.3
  94.5 46.2 all-gather.5
  142.7 110.9 all-gather.7
  296.5 39.4 reduce-scatter.1

commit v3 on v2

--- a/solution.py
+++ b/solution.py
@@ -147,6 +147,43 @@
     )(tokens, routes_t, low_t)
 
 
+def row_kernel(nrow, total, out, own_sem, send, recv):
+    row, col = lax.axis_index("row"), lax.axis_index("col")
+    width = out.shape[2]
+    greet(nrow, 1, row, col)
+
+    def part(there):
+        return total.at[:, pl.ds(pl.multiple_of(there * width, width), width)]
+
+    copies = []
+    for k in range(1, nrow):
+        there = lax.rem(row + k, nrow)
+        copies.append(remote(part(there), out.at[row], send.at[k], recv.at[row], there, col))
+        copies[-1].start()
+    own = pltpu.make_async_copy(part(row), out.at[row], own_sem)
+    own.start()
+    own.wait()
+    for k in range(1, nrow):
+        there = lax.rem(row + k, nrow)
+        remote(part(there), out.at[there], send.at[k], recv.at[there], there, col).wait_recv()
+    for copy in copies:
+        copy.wait_send()
+
+
+def exchange_rows(total, width):
+    nrow = lax.axis_size("row")
+    dma = pltpu.SemaphoreType.DMA
+    return pl.pallas_call(
+        functools.partial(row_kernel, nrow),
+        out_shape=jax.ShapeDtypeStruct((nrow, total.shape[0], width), total.dtype),
+        in_specs=[pl.BlockSpec(memory_space=pl.ANY)],
+        out_specs=pl.BlockSpec(memory_space=pl.ANY),
+        scratch_shapes=[dma, dma((nrow,)), dma((nrow,))],
+        compiler_params=pltpu.CompilerParams(collective_id=1, has_side_effects=True),
+        name="exchange_rows",
+    )(total)
+
+
 def on_device(
     tokens,
     router,
@@ -227,7 +264,9 @@
     weight_of = jnp.sum(jnp.where(onehot, gate_weights[:, :, None], 0.0), axis=1)
     slots = jnp.arange(capacity, dtype=jnp.int32)
     here = hit[:, :, None] & (rank_own[:, :, None] == slots[None, None, :])
-    combine = jnp.where(here, weight_of[:, :, None], 0.0).reshape(token_count, expert_count * capacity)
+    combine = jnp.where(here, weight_of[:, :, None], 0.0).reshape(
+        token_count, col_count, local_experts, capacity
+    )
     combine_hi = combine.astype(BF)
     combine_lo = (combine - combine_hi.astype(F32)).astype(BF)
 
@@ -241,27 +280,31 @@
         .astype(BF)
         .transpose(2, 0, 3, 1)
     )
-    rows = jnp.einsum("egst,gtd->egsd", pick, all_tokens, preferred_element_type=F32).astype(BF)
-    rows = rows.reshape(local_experts, col_count * capacity, full_width)
-    gate_part = jnp.einsum("esd,edf->esf", rows, routed_gate_weight, preferred_element_type=F32)
-    up_part = jnp.einsum("esd,edf->esf", rows, routed_up_weight, preferred_element_type=F32)
-    hidden = (jax.nn.silu(gate_part) * up_part).astype(BF)
-    partial = jnp.einsum(
-        "esf,efd->esd", hidden, routed_down_weight, preferred_element_type=F32
-    ).astype(BF)
-    outgoing = partial.reshape(local_experts, col_count, capacity, full_width).transpose(1, 0, 2, 3)
-    returned = lax.all_to_all(outgoing, "col", split_axis=0, concat_axis=0, tiled=True)
-    flat = returned.reshape(expert_count * capacity, full_width)
+    flats = []
+    for e in range(local_experts):
+        rows = jnp.einsum("gst,gtd->gsd", pick[e], all_tokens, preferred_element_type=F32)
+        rows = rows.astype(BF).reshape(col_count * capacity, full_width)
+        gate_part = dot(rows, routed_gate_weight[e])
+        up_part = dot(rows, routed_up_weight[e])
+        hidden = (jax.nn.silu(gate_part) * up_part).astype(BF)
+        partial = dot(hidden, routed_down_weight[e]).astype(BF)
+        outgoing = partial.reshape(col_count, capacity, full_width)
+        returned = lax.all_to_all(outgoing, "col", split_axis=0, concat_axis=0, tiled=True)
+        flats.append(returned.reshape(col_count * capacity, full_width))
 
     shared_gate_value = dot(all_features, gate_full)
     shared_up_value = dot(all_features, up_full)
     shared_hidden = (
         jax.nn.silu(shared_gate_value) * (shared_up_value + ADAPTER_SCALE * delta)
     ).astype(BF)
-    shared_part = dot(shared_hidden, down_full) * share[:, None]
-
-    total = dot(combine_hi, flat) + dot(combine_lo, flat) + shared_part
-    return lax.psum_scatter(total, "row", scatter_dimension=1, tiled=True)
+    shared_hidden, combine_hi, combine_lo = lax.optimization_barrier(
+        (shared_hidden, combine_hi, combine_lo)
+    )
+    total = dot(shared_hidden, down_full) * share[:, None]
+    for e in range(local_experts):
+        for part in (combine_hi, combine_lo):
+            total = total + dot(part[:, :, e].reshape(token_count, col_count * capacity), flats[e])
+    return jnp.sum(exchange_rows(total.astype(BF), local_width).astype(F32), axis=0)
 
 
 def solution(mesh):

time: 347 us -> 320 us (0.922); the launches traced: 343 us -> 319 us
  waiting for transfers between devices: 139 us -> 90.5 us
  Pallas kernels: 82.1 us -> 109 us
  local copies, waits for them, and re-layouts: 20.2 us -> 8.51 us
  starting transfers between devices: 5.89 us -> 11.6 us
  matrix products: 70.4 us -> 75.9 us
    all_to_all x1 -> x2, waiting for transfers between devices: 97.5 us -> 30.7 us  [on_device(): lax.all_to_all(outgoing, 'col', split_axis=0, concat_axis=0, tiled=True)]
    all_gather x1, waiting for transfers between devices: 0.02 us -> 57.7 us  [on_device(): down_full = lax.all_gather(shared_down_weight, 'col', axis=1, tiled=True)]
    reduce_scatter x1 -> x0, waiting for transfers between devices: 39.6 us -> none  [on_device(): return lax.psum_scatter(total, 'row', scatter_dimension=1, tiled=True)]
    pallas_call x0 -> x1, Pallas kernels: none -> 26.5 us  [exchange_rows(): pl.pallas_call(functools.partial(row_kernel, nrow), out_shape=jax.ShapeDt...]
    dot_general x8 -> x15, matrix products: 36.2 us -> 62.6 us  [dot(): return jnp.dot(a, b, preferred_element_type=F32)]
    dot_general x3 -> x2, matrix products: 31.2 us -> 10.3 us  [on_device(): jnp.einsum('gst,gtd->gsd', pick[e], all_tokens, preferred_element_type=F32)]
    convert_element_type x3 -> x0, local copies, waits for them, and re-layouts: 8.56 us -> none  [the longest x1 8.4 us: on_device(): jnp.einsum('egst,gtd->egsd', pick, all_tokens, preferred_element_type=F32)]
    reshape x1 -> x0, local copies, waits for them, and re-layouts: 8.26 us -> none  [on_device(): partial.reshape(local_experts, col_count, capacity, full_width)]
  transfers between devices with their start and end apart: 5 -> 5, of which waited for: 2 -> 2; matrix products, arithmetic and copies ran while one was open for 24% -> 25% of each run, Pallas kernels for 24% -> 26%
where the time goes in v3:
time: 320 us; the launch traced here: 319 us
  Pallas kernels  109 us (34%)
  waiting for transfers between devices  90.5 us (28%)
  matrix products  75.9 us (24%)
  between operations  13.4 us (4%)
  starting transfers between devices  11.6 us (4%)
  other arithmetic  10.6 us (3%)
  local copies, waits for them, and re-layouts  8.51 us (3%)
    pallas_call x1, Pallas kernels, gather_tokens(): pl.pallas_call(functools.partial(gather_kernel, nrow, ncol), out_shape=(j...  82.1 us
    dot_general x15, matrix products, dot(): return jnp.dot(a, b, preferred_element_type=F32)  62.6 us
    all_gather x1, waiting for transfers between devices, on_device(): down_full = lax.all_gather(shared_down_weight, 'col', axis=1, tiled=True)  57.7 us
    all_to_all x2, waiting for transfers between devices, on_device(): lax.all_to_all(outgoing, 'col', split_axis=0, concat_axis=0, tiled=True)  30.7 us
    pallas_call x1, Pallas kernels, exchange_rows(): pl.pallas_call(functools.partial(row_kernel, nrow), out_shape=jax.ShapeDt...  26.5 us
    all_to_all x2, starting transfers between devices, on_device(): lax.all_to_all(outgoing, 'col', split_axis=0, concat_axis=0, tiled=True)  11.6 us
    dot_general x2, matrix products, on_device(): jnp.einsum('gst,gtd->gsd', pick[e], all_tokens, preferred_element_type=F32)  10.3 us
  transfers between devices with their start and end apart: 5, of which 2 were waited for; matrix products, arithmetic and copies ran while one was open for 25% of the time, Pallas kernels for 26%

profile of v3, /device:TPU:11, one launch (start us, length us, event | category | flops | bytes accessed | tf_op | source)
XLA Modules:
  0.0 319.2 jit_solution(1552821419969981901)
XLA Ops:
  6.5 0.0 copy-start
  6.5 0.0 all-gather.4.cloned.1.call-start
  6.5 0.7 all-gather.4.cloned.1.call-update
  7.3 0.0 all-gather.6.cloned.1.call-start
  7.3 0.7 all-gather.6.cloned.1.call-update
  8.0 0.0 all-gather.8.cloned.1.call-start
  8.1 0.7 all-gather.8.cloned.1.call-update
  8.7 0.0 copy-start.10
  8.8 0.7 select_reduce_fusion.4
  9.5 0.1 convert_reduce_fusion.1
  9.6 0.9 select_reduce_fusion.3
  10.5 0.1 select_reduce_fusion.2
  10.5 2.8 convolution_select_fusion
  13.3 2.6 copy.27
  15.9 1.9 reduce_sum.94
  17.8 0.0 copy-done.10
  17.8 0.6 pad.4.rts
  18.4 82.1 %gather_tokens.1 = (bf16[8,256,2048]{2,1,0:T(8,128)(2,1)}, s32[8,8,256]{2,1,0:T(8,128)}, f32[4,16,256]{2,1,0:T(8,128)}) custom-call(bf16[256,512]{1,0:T(8,128)(2,1)} %tok.1, s32[8,256]{1,0:T(8,128)} %pad.4.rts, f32[16,256]{1,0:T(8,128)} %bitcast.118), custom_call_target="tpu_custom_call" | custom-call | bytes 83886080 | tf_op jit(solution)/shard_map/gather_tokens/pallas_call | solution.py:129
  100.6 1.0 compare_reduce_fusion
  101.6 0.2 fusion.41
  101.7 0.4 fusion.20
  102.1 0.0 copy-start.12
  102.1 5.3 %convolution_convert_fusion.3 = bf16[8,128,2048]{2,1,0:T(8,128)(2,1)S(1)} fusion(bf16[8,256,2048]{2,1,0:T(8,128)(2,1)} %get-tuple-element.11, pred[2,8,128,256]{3,2,1,0:T(32,128)(4,1)S(1)} %fusion.20), kind=kOutput, calls=%fused_computation.3 | convolution fusion | flops 1075838976 | bytes 12845056 | tf_op jit(solution)/shard_map/gst,gtd->gsd/dot_general | solution.py:285
  107.4 0.0 copy-start.2
  107.5 2.0 copy-done.2
  109.4 0.0 copy-done.12
  109.4 2.8 fusion.27
  112.3 9.5 %convolution_convert_fusion.2 = bf16[1024,2048]{1,0:T(8,128)(2,1)} fusion(bf16[2,352,2048]{2,1,0:T(8,128)(2,1)} %param.23, bf16[1024,2048]{1,0:T(8,128)(2,1)} %bitcast.109, bf16[2,2048,352]{1,2,0:T(8,128)(2,1)} %param.22, f32[1024,352]{0,1:T(8,128)} %fusion.27), kind=kOutput, calls=%fused_computation.2 | convolution fusion | flops 2957049856 | bytes 12713984 | tf_op jit(solution)/shard_map/dot_general | solution.py:16
  121.8 5.3 %all-to-all-start = ((bf16[8,128,2048]{2,1,0:T(8,128)(2,1)}), bf16[8,128,2048]{2,1,0:T(8,128)(2,1)}, u32[]{:S(2)}, u32[]{:S(2)}) async-start(bf16[8,128,2048]{2,1,0:T(8,128)(2,1)} %bitcast.111), calls=%async_computation | async-start | bytes 8388608 | tf_op jit(solution)/shard_map/all_to_all | solution.py:292
  127.0 0.0 copy-done.8
  127.0 1.6 fusion.44
  128.8 0.2 convolution_convert_fusion.5
  129.0 0.0 copy-done.11
  129.1 1.6 fusion.42
  130.7 1.6 fusion.18
  132.3 1.7 select_convert_fusion
  133.9 5.0 %convolution_convert_fusion.1 = bf16[8,128,2048]{2,1,0:T(8,128)(2,1)S(1)} fusion(bf16[8,256,2048]{2,1,0:T(8,128)(2,1)} %get-tuple-element.11, pred[2,8,128,256]{3,2,1,0:T(32,128)(4,1)S(1)} %fusion.20), kind=kOutput, calls=%fused_computation.1 | convolution fusion | flops 1075838976 | bytes 12845056 | tf_op jit(solution)/shard_map/gst,gtd->gsd/dot_general | solution.py:285
  138.9 0.0 copy-start.1
  138.9 2.0 copy-done.1
  140.9 0.0 copy-done.13
  140.9 2.8 fusion.23
  143.7 9.4 %convolution_convert_fusion = bf16[1024,2048]{1,0:T(8,128)(2,1)} fusion(bf16[2,352,2048]{2,1,0:T(8,128)(2,1)} %param.23, bf16[1024,2048]{1,0:T(8,128)(2,1)} %bitcast.107, bf16[2,2048,352]{1,2,0:T(8,128)(2,1)} %param.22, f32[1024,352]{0,1:T(8,128)} %fusion.23), kind=kOutput, calls=%fused_computation | convolution fusion | flops 2957049856 | bytes 12713984 | tf_op jit(solution)/shard_map/dot_general | solution.py:16
  153.1 30.7 %all-to-all-done = bf16[8,128,2048]{2,1,0:T(8,128)(2,1)} async-done(((bf16[8,128,2048]{2,1,0:T(8,128)(2,1)}), bf16[8,128,2048]{2,1,0:T(8,128)(2,1)}, u32[]{:S(2)}, u32[]{:S(2)}) %all-to-all-start) | async-done | bytes 4194336 | tf_op jit(solution)/shard_map/all_to_all | solution.py:292
  183.8 6.3 %all-to-all-start.1 = ((bf16[8,128,2048]{2,1,0:T(8,128)(2,1)}), bf16[8,128,2048]{2,1,0:T(8,128)(2,1)}, u32[]{:S(2)}, u32[]{:S(2)}) async-start(bf16[8,128,2048]{2,1,0:T(8,128)(2,1)} %bitcast.110), calls=%async_computation.1 | async-start | bytes 8388608 | tf_op jit(solution)/shard_map/all_to_all | solution.py:292
  190.1 0.0 copy-done.9
  190.2 0.0 all-gather.4.cloned.1.call-done
  190.2 5.9 %fusion.48 = f32[256,1408]{1,0:T(8,128)} fusion(bf16[2048,1408]{1,0:T(8,128)(2,1)} %all-gather.4.cloned.1.call-done, bf16[8,256,2048]{2,1,0:T(8,128)(2,1)} %get-tuple-element.11, s32[]{:T(128)S(6)} %select_n.59), kind=kOutput, calls=%fused_computation.53 | convolution fusion | flops 1476395008 | bytes 8257540 | tf_op jit(solution)/shard_map/dot_general | solution.py:16
  196.1 4.9 %fusion.46 = f32[256,1408]{1,0:T(8,128)S(1)} fusion(bf16[2048,1408]{1,0:T(8,128)(2,1)} %all-gather.6.cloned.1.call-done, bf16[8,256,2048]{2,1,0:T(8,128)(2,1)} %get-tuple-element.11, s32[]{:T(128)S(6)} %select_n.59), kind=kOutput, calls=%fused_computation.51 | convolution fusion | flops 1476395008 | bytes 8257540 | tf_op jit(solution)/shard_map/dot_general | solution.py:16
  201.0 0.0 copy-done
  201.0 0.0 copy-done.14
  201.0 0.0 copy-start.3
  201.0 0.0 copy-start.4
  201.0 2.3 fusion.14
  203.3 0.0 copy-done.3
  203.3 1.2 fusion.79
  204.5 57.7 %all-gather.8.cloned.1.call-done = bf16[1408,2048]{1,0:T(8,128)(2,1)} async-done(((bf16[1408,256]{1,0:T(8,128)(2,1)}), bf16[1408,2048]{1,0:T(8,128)(2,1)}) %all-gather.8.cloned.1.call-update) | async-done | bytes 5767184 | tf_op jit(solution)/shard_map/all_gather | solution.py:216
  262.2 4.7 %convolution_multiply_fusion = f32[256,2048]{1,0:T(8,128)S(1)} fusion(bf16[256,1408]{1,0:T(8,128)(2,1)} %fusion.14, bf16[1408,2048]{1,0:T(8,128)(2,1)} %all-gather.8.cloned.1.call-done, f32[256]{0:T(256)S(1)} %add_divide_fusion), kind=kOutput, calls=%fused_computation.10 | convolution fusion | flops 1476919296 | bytes 8586240 | tf_op jit(solution)/shard_map/dot_general | solution.py:16
  266.9 3.5 %convolution_add_fusion.3 = f32[256,2048]{1,0:T(8,128)S(1)} fusion(f32[256,2048]{1,0:T(8,128)S(1)} %convolution_multiply_fusion, bf16[256,1024]{0,1:T(8,128)(2,1)S(1)} %bitcast.115, bf16[1024,2048]{1,0:T(8,128)(2,1)} %bitcast.20), kind=kOutput, calls=%fused_computation.16 | convolution fusion | flops 1074266112 | bytes 8912896 | tf_op jit(solution)/shard_map/dot_general | solution.py:16
  270.4 4.8 %convolution_add_fusion.2 = f32[256,2048]{1,0:T(8,128)} fusion(f32[256,2048]{1,0:T(8,128)S(1)} %convolution_add_fusion.3, bf16[256,1024]{0,1:T(8,128)(2,1)S(1)} %bitcast.114, bf16[1024,2048]{1,0:T(8,128)(2,1)} %bitcast.20), kind=kOutput, calls=%fused_computation.15 | convolution fusion | flops 1074266112 | bytes 8912896 | tf_op jit(solution)/shard_map/dot_general | solution.py:16
  275.3 0.0 all-to-all-done.1
  275.3 4.2 %convolution_add_fusion.1 = f32[256,2048]{1,0:T(8,128)S(1)} fusion(f32[256,2048]{1,0:T(8,128)} %convolution_add_fusion.2, bf16[256,1024]{0,1:T(8,128)(2,1)S(1)} %bitcast.113, bf16[1024,2048]{1,0:T(8,128)(2,1)} %bitcast.29), kind=kOutput, calls=%fused_computation.14 | convolution fusion | flops 1074266112 | bytes 8912896 | tf_op jit(solution)/shard_map/dot_general | solution.py:16
  279.5 4.5 %fusion.17.total = bf16[256,2048]{1,0:T(8,128)(2,1)} fusion(f32[256,2048]{1,0:T(8,128)S(1)} %convolution_add_fusion.1, bf16[256,1024]{0,1:T(8,128)(2,1)S(1)} %bitcast.117, bf16[1024,2048]{1,0:T(8,128)(2,1)} %bitcast.29), kind=kOutput, calls=%fused_computation.18 | convolution fusion | flops 1074790400 | bytes 7864320 | tf_op jit(solution)/shard_map/dot_general | solution.py:16
  284.0 26.5 %exchange_rows.1 = bf16[4,256,512]{2,1,0:T(8,128)(2,1)} custom-call(bf16[256,2048]{1,0:T(8,128)(2,1)} %fusion.17.total), custom_call_target="tpu_custom_call" | custom-call | tf_op jit(solution)/shard_map/exchange_rows/pallas_call | solution.py:176
  310.5 2.2 convert_reduce_fusion
  (31 shorter events, 0.3 us)
Async XLA Ops:
  6.5 194.4 %copy-start = (bf16[64,16,1408]{2,1,0:T(8,128)(2,1)S(1)}, bf16[64,16,1408]{2,1,0:T(8,128)(2,1)}, u32[]{:S(2)}) copy-start(bf16[64,16,1408]{2,1,0:T(8,128)(2,1)} %param.25) | copy-start | bytes 8650756
  6.5 183.7 %all-gather.4.cloned.1.call-start = ((), (), s32[]{:S(2)}) async-start(), calls=%async_computation.2 | async-start | bytes 6488064 | tf_op jit(solution)/shard_map/all_gather | solution.py:214
  7.3 188.9 %all-gather.6.cloned.1.call-start = ((), (), s32[]{:S(2)}) async-start(), calls=%async_computation.3 | async-start | bytes 6488064 | tf_op jit(solution)/shard_map/all_gather | solution.py:215
  8.0 254.1 %all-gather.8.cloned.1.call-start = ((), (), s32[]{:S(2)}) async-start(), calls=%async_computation.4 | async-start | bytes 6488064 | tf_op jit(solution)/shard_map/all_gather | solution.py:216
  8.7 9.1 %copy-start.10 = (s32[256,4]{0,1:T(4,128)S(1)}, s32[256,4]{0,1:T(4,128)}, u32[]{:S(2)}) copy-start(s32[256,4]{0,1:T(4,128)} %param.26) | copy-start | bytes 12292
  102.1 7.3 %copy-start.12 = (bf16[2,2048,352]{1,2,0:T(8,128)(2,1)S(1)}, bf16[2,2048,352]{1,2,0:T(8,128)(2,1)}, u32[]{:S(2)}) copy-start(bf16[2,2048,352]{1,2,0:T(8,128)(2,1)} %param.21) | copy-start | bytes 8650756
  107.4 2.0 copy-start.2
  121.8 5.3 %copy-start.8 = (bf16[2048,16]{0,1:T(8,128)(2,1)S(1)}, bf16[2048,16]{0,1:T(8,128)(2,1)}, u32[]{:S(2)}) copy-start(bf16[2048,16]{0,1:T(8,128)(2,1)} %param.16) | copy-start | bytes 196612
  121.8 7.3 %copy-start.11 = (bf16[2048]{0:T(1024)(128)(2,1)S(1)}, bf16[2048]{0:T(1024)(128)(2,1)}, u32[]{:S(2)}) copy-start(bf16[2048]{0:T(1024)(128)(2,1)} %param.17) | copy-start | bytes 12292
  121.8 62.1 %all-to-all-start = ((bf16[8,128,2048]{2,1,0:T(8,128)(2,1)}), bf16[8,128,2048]{2,1,0:T(8,128)(2,1)}, u32[]{:S(2)}, u32[]{:S(2)}) async-start(bf16[8,128,2048]{2,1,0:T(8,128)(2,1)} %bitcast.111), calls=%async_computation | async-start | bytes 8388608 | tf_op jit(solution)/shard_map/all_to_all | solution.py:292
  133.9 7.0 %copy-start.13 = (bf16[2,2048,352]{1,2,0:T(8,128)(2,1)S(1)}, bf16[2,2048,352]{1,2,0:T(8,128)(2,1)}, u32[]{:S(2)}) copy-start(bf16[2,2048,352]{1,2,0:T(8,128)(2,1)} %param.21) | copy-start | bytes 8650756
  138.9 2.0 copy-start.1
  183.8 6.3 %copy-start.9 = (f32[4,16,256]{2,1,0:T(8,128)S(1)}, f32[4,16,256]{2,1,0:T(8,128)}, u32[]{:S(2)}) copy-start(f32[4,16,256]{2,1,0:T(8,128)} %get-tuple-element.12) | copy-start | bytes 196612
  183.8 91.5 %all-to-all-start.1 = ((bf16[8,128,2048]{2,1,0:T(8,128)(2,1)}), bf16[8,128,2048]{2,1,0:T(8,128)(2,1)}, u32[]{:S(2)}, u32[]{:S(2)}) async-start(bf16[8,128,2048]{2,1,0:T(8,128)(2,1)} %bitcast.110), calls=%async_computation.1 | async-start | bytes 8388608 | tf_op jit(solution)/shard_map/all_to_all | solution.py:292
  196.1 4.9 %copy-start.14 = (f32[256,1408]{1,0:T(8,128)S(1)}, f32[256,1408]{1,0:T(8,128)}, u32[]{:S(2)}) copy-start(f32[256,1408]{1,0:T(8,128)} %fusion.48) | copy-start | bytes 4325380
  201.0 2.3 copy-start.3
  201.0 2.3 copy-start.4
  262.2 4.7 %copy-start.6 = (bf16[256,8,1,128]{0,3,1,2:T(8,128)(2,1)S(1)}, bf16[256,8,1,128]{0,3,1,2:T(8,128)(2,1)}, u32[]{:S(2)}) copy-start(bf16[256,8,1,128]{0,3,1,2:T(8,128)(2,1)} %get-tuple-element.21) | copy-start | bytes 1572868
  266.9 3.6 %copy-start.5 = (bf16[256,8,1,128]{0,3,1,2:T(8,128)(2,1)S(1)}, bf16[256,8,1,128]{0,3,1,2:T(8,128)(2,1)}, u32[]{:S(2)}) copy-start(bf16[256,8,1,128]{0,3,1,2:T(8,128)(2,1)} %get-tuple-element.18) | copy-start | bytes 1572868
  275.3 4.2 %copy-start.7 = (bf16[256,8,1,128]{0,3,1,2:T(8,128)(2,1)S(1)}, bf16[256,8,1,128]{0,3,1,2:T(8,128)(2,1)}, u32[]{:S(2)}) copy-start(bf16[256,8,1,128]{0,3,1,2:T(8,128)(2,1)} %get-tuple-element.17) | copy-start | bytes 1572868
Sparse Core Ops, SparseCore 0:
  9.2 83.6 all-gather.3
  94.8 66.5 all-gather.5
  163.3 98.7 all-gather.7
